TPU v7x, 32 devices: a whole 2x2x4 slice. The times are simulated.
32 devices in a mesh: row: 8 (over y, x, core), col: 4 (over z).
Axes of the slice: x: 2, y: 2, z: 4, core: 2. Of those that a mesh axis runs over, the one named last changes fastest.
Arguments:
- kernel: float32 [5120, 5120], P('row', 'col'), as said below
Outputs:
- factored: float32 [5120, 5120], P('row', 'col')
Inputs may be any that keep to these rules, and one draw needn't show every extreme that they name: `kernel`: in global order symmetric positive definite; its eigenvalues are at least 0.05.
All inputs are finite; a program needn't handle non-finite values.
Results may differ from a plain program's by a relative error of at most 0.0003.
Values sent between devices are 32-bit elements; how exact they have to be, the bound alone decides.
A program may use at most 128 MiB of HBM per device.

v0:
```python
import jax
import jax.numpy as jnp
from jax import lax
from jax.sharding import PartitionSpec as P

NB = 128


def broadcast(value, axis, source):
    kept = jnp.where(lax.axis_index(axis) == source, value, 0).astype(value.dtype)
    return lax.psum(kept, axis)


def local(kernel):
    rows_here, cols_here = kernel.shape
    nrow = lax.axis_size("row")
    ncol = lax.axis_size("col")
    row_idx = lax.axis_index("row")
    col_idx = lax.axis_index("col")
    blocks_r = rows_here // NB
    blocks_c = cols_here // NB
    groups = nrow // ncol
    rows_g = jnp.arange(blocks_r, dtype=jnp.int32) * nrow + row_idx
    cols_g = jnp.arange(blocks_c, dtype=jnp.int32) * ncol + col_idx

    def factor_panel(matrix, step):
        start_r = step // nrow * NB
        start_c = step // ncol * NB
        corner = matrix[start_r : start_r + NB, start_c : start_c + NB]
        corner = broadcast(corner, "row", step % nrow)
        lower = jnp.linalg.cholesky(corner)
        inverse = lax.linalg.triangular_solve(
            lower, jnp.eye(NB, dtype=lower.dtype), left_side=True, lower=True
        )
        column = matrix[:, start_c : start_c + NB]
        solved = jnp.dot(column, inverse.T, precision=lax.Precision.HIGHEST).reshape(
            blocks_r, NB, NB
        )
        panel = jnp.where(
            (rows_g < step)[:, None, None],
            jnp.float32(0.0),
            jnp.where((rows_g == step)[:, None, None], lower[None], solved),
        )
        panel = panel.reshape(rows_here, NB)
        rows_side = broadcast(panel, "col", step % ncol)
        whole = lax.all_gather(rows_side, "row", axis=0, tiled=True)
        stacked = whole.reshape(groups, ncol, blocks_r, NB, NB)
        picked = lax.dynamic_index_in_dim(stacked, col_idx, 1, keepdims=False)
        cols_side = picked.transpose(1, 0, 2, 3).reshape(cols_here, NB)
        return (rows_side, cols_side)

    def product(left, right):
        return jnp.dot(left, right.T, precision=lax.Precision.HIGHEST)

    rows_first, cols_first = factor_panel(kernel, 0)
    updated = kernel - product(rows_first, cols_first)
    rows_second, cols_second = factor_panel(updated, 1)
    updated = updated - product(rows_second, cols_second)
    row_mask = jnp.repeat(rows_g < 2, NB)
    col_mask = jnp.repeat(cols_g >= 2, NB)
    result = jnp.where(row_mask[:, None] & col_mask[None, :], jnp.float32(0.0), updated)
    for step, rows_side in ((0, rows_first), (1, rows_second)):
        start_c = step // ncol * NB
        current = result[:, start_c : start_c + NB]
        chosen = jnp.where(col_idx == step % ncol, rows_side, current)
        result = lax.dynamic_update_slice(result, chosen, (0, start_c))
    return result


def solution(mesh):
    return jax.shard_map(
        local,
        mesh=mesh,
        in_specs=(P("row", "col"),),
        out_specs=P("row", "col"),
        check_vma=False,
    )
```

profile of v0, /device:TPU:20, one launch (start us, length us, event | category | flops | bytes accessed | tf_op | source)
XLA Modules:
  0.0 341.1 jit_solution(4612267742167517512)
XLA Ops:
  6.5 3.5 %copy.29 = f32[640,1280]{0,1:T(8,128)S(1)} copy(f32[640,1280]{1,0:T(8,128)} %param.4) | data formatting | bytes 6553600 | tf_op args[0]
  10.9 52.8 %all-reduce.5.cloned.1.call-done = f32[128,128]{0,1:T(8,128)} async-done(((f32[128,128]{0,1:T(8,128)}), f32[128,128]{0,1:T(8,128)}) %all-reduce.5.cloned.1.call-update) | async-done | bytes 65552 | tf_op jit(solution)/shard_map/psum | solution.py:11
  63.7 0.9 copy.25
  65.5 11.7 %cholesky.44 = f32[128,128]{1,0:T(8,128)S(1)} custom-call(f32[128,128]{1,0:T(8,128)S(1)} %fusion.16), custom_call_target="Cholesky" | custom-call | tf_op jit(solution)/shard_map/jit(cholesky)/cholesky | solution.py:31
  78.6 9.8 %custom-call.6 = f32[1,128,128]{1,2,0:T(8,128)S(1)} custom-call(f32[1,128,128]{2,1,0:T(8,128)S(1)} %get-tuple-element.9), custom_call_target="InvertDiagBlocksLowerTriangular" | custom-call | tf_op jit(solution)/shard_map/triangular_solve/custom-call.0 | solution.py:32
  89.4 1.9 copy.26
  91.3 2.3 fusion.3
  93.7 36.0 %all-reduce.7.cloned.1.call-done = f32[640,128]{0,1:T(8,128)} async-done(((f32[640,128]{0,1:T(8,128)}), f32[640,128]{0,1:T(8,128)}) %all-reduce.7.cloned.1.call-update) | async-done | bytes 327696 | tf_op jit(solution)/shard_map/psum | solution.py:11
  129.9 32.0 %all-gather.3.cloned.1.call-done = f32[5120,128]{0,1:T(8,128)} async-done(((f32[640,128]{0,1:T(8,128)}), f32[5120,128]{0,1:T(8,128)}) %all-gather.3.cloned.1.call-update) | async-done | bytes 2621456 | tf_op jit(solution)/shard_map/all_gather | solution.py:46
  161.9 3.2 copy.27
  165.2 1.1 dynamic-slice_bitcast_fusion.1
  166.4 4.8 %convolution_subtract_fusion.1 = f32[640,1280]{0,1:T(8,128)S(1)} fusion(f32[640,1280]{0,1:T(8,128)} %copy-done, f32[640,128]{0,1:T(8,128)} %all-reduce.7.cloned.1.call-done, f32[1280,128]{1,0:T(8,128)S(1)} %bitcast.61), kind=kOutput, calls=%fused_computation.2 | convolution fusion | flops 1259110400 | bytes 7536640 | tf_op jit(solution)/shard_map/dot_general | solution.py:53
  172.2 51.7 %all-reduce.9.cloned.1.call-done = f32[128,128]{0,1:T(8,128)} async-done(((f32[128,128]{0,1:T(8,128)}), f32[128,128]{0,1:T(8,128)}) %all-reduce.9.cloned.1.call-update) | async-done | bytes 65552 | tf_op jit(solution)/shard_map/psum | solution.py:11
  223.9 0.9 copy.31
  225.7 11.7 %cholesky.55 = f32[128,128]{1,0:T(8,128)S(1)} custom-call(f32[128,128]{1,0:T(8,128)S(1)} %fusion.14), custom_call_target="Cholesky" | custom-call | tf_op jit(solution)/shard_map/jit(cholesky)/cholesky | solution.py:31
  238.8 9.8 %custom-call.7 = f32[1,128,128]{1,2,0:T(8,128)S(1)} custom-call(f32[1,128,128]{2,1,0:T(8,128)S(1)} %get-tuple-element.6), custom_call_target="InvertDiagBlocksLowerTriangular" | custom-call | tf_op jit(solution)/shard_map/triangular_solve/custom-call.0 | solution.py:32
  249.6 1.9 copy.32
  251.5 2.1 fusion.5
  253.7 36.0 %all-reduce.11.cloned.1.call-done = f32[640,128]{0,1:T(8,128)} async-done(((f32[640,128]{0,1:T(8,128)}), f32[640,128]{0,1:T(8,128)}) %all-reduce.11.cloned.1.call-update) | async-done | bytes 327696 | tf_op jit(solution)/shard_map/psum | solution.py:11
  289.9 31.7 %all-gather.5.cloned.1.call-done = f32[5120,128]{0,1:T(8,128)} async-done(((f32[640,128]{0,1:T(8,128)}), f32[5120,128]{0,1:T(8,128)}) %all-gather.5.cloned.1.call-update) | async-done | bytes 2621456 | tf_op jit(solution)/shard_map/all_gather | solution.py:46
  321.6 3.2 copy.34
  324.8 1.1 dynamic-slice_bitcast_fusion
  326.0 4.2 %fusion = f32[640,1280]{0,1:T(8,128)S(1)} fusion(f32[640,1280]{0,1:T(8,128)S(1)} %convolution_subtract_fusion.1, f32[640,128]{0,1:T(8,128)} %all-reduce.11.cloned.1.call-done, f32[1280,128]{1,0:T(8,128)S(1)} %bitcast.60, pred[640]{0:T(1024)(128)(4,1)S(1)} %broadcast_bitcast_fusion.5, pred[1280]{0:T(1024)(128)(4,1)S(1)} %broadcast_bitcast_fusion), kind=kOutput, calls=%fused_computation.1 | convolution fusion | flops 1260748800 | bytes 7538560 | tf_op jit(solution)/shard_map/dot_general | solution.py:53
  331.3 3.0 copy.37
  (47 shorter events, 9.9 us)
Async XLA Ops:
  6.5 57.2 %all-reduce.5.cloned.1.call-start = ((), (), s32[]{:S(2)}) async-start(), calls=%async_computation | async-start | bytes 131072 | tf_op jit(solution)/shard_map/psum | solution.py:11
  10.0 155.2 %copy-start = (f32[640,1280]{0,1:T(8,128)}, f32[640,1280]{0,1:T(8,128)S(1)}, u32[]{:S(2)}) copy-start(f32[640,1280]{0,1:T(8,128)S(1)} %copy.29) | copy-start | bytes 9830404
  10.7 119.0 %all-reduce.7.cloned.1.call-start = ((), (), s32[]{:S(2)}) async-start(), calls=%async_computation.1 | async-start | bytes 655360 | tf_op jit(solution)/shard_map/psum | solution.py:11
  93.6 68.3 %all-gather.3.cloned.1.call-start = ((), (), s32[]{:S(2)}) async-start(), calls=%async_computation.2 | async-start | bytes 2949120 | tf_op jit(solution)/shard_map/all_gather | solution.py:46
  129.7 94.2 %all-reduce.9.cloned.1.call-start = ((), (), s32[]{:S(2)}) async-start(), calls=%async_computation.3 | async-start | bytes 131072 | tf_op jit(solution)/shard_map/psum | solution.py:11
  171.9 117.9 %all-reduce.11.cloned.1.call-start = ((), (), s32[]{:S(2)}) async-start(), calls=%async_computation.4 | async-start | bytes 655360 | tf_op jit(solution)/shard_map/psum | solution.py:11
  253.6 68.0 %all-gather.5.cloned.1.call-start = ((), (), s32[]{:S(2)}) async-start(), calls=%async_computation.5 | async-start | bytes 2949120 | tf_op jit(solution)/shard_map/all_gather | solution.py:46
  330.2 1.0 copy-start.1
  330.2 1.1 copy-start.2
Sparse Core Ops, SparseCore 0:
  10.8 52.8 all-reduce.4
  93.7 35.9 all-reduce.6
  131.8 30.0 all-gather.2
  172.0 51.8 all-reduce.8
  253.8 35.9 all-reduce.10
  291.5 30.0 all-gather.4
where the time goes:
time: 344 us; the launch traced here: 341 us
  waiting for transfers between devices  240 us (70%)
  other arithmetic  48.9 us (14%)
  local copies, waits for them, and re-layouts  23.7 us (7%)
  matrix products  14 us (4%)
  between operations  13.7 us (4%)
    psum x4, waiting for transfers between devices, broadcast(): return lax.psum(kept, axis)  177 us
    all_gather x2, waiting for transfers between devices, factor_panel(): whole = lax.all_gather(rows_side, 'row', axis=0, tiled=True)  63.7 us
    another operation x6, other arithmetic, factor_panel(): lower = jnp.linalg.cholesky(corner)  24.8 us
    another operation x4, other arithmetic, factor_panel(): lax.linalg.triangular_solve(lower, jnp.eye(NB, dtype=lower.dtype), left_s...  20.9 us
    dot_general x2, matrix products, product(): return jnp.dot(left, right.T, precision=lax.Precision.HIGHEST)  8.99 us
  transfers between devices with their start and end apart: 6, of which 6 were waited for; matrix products, arithmetic and copies ran while one was open for 0% of the time, Pallas kernels for 0%

commit v1 on v0

v1 whole, which is shorter than its diff:
```python
import functools
import math

import jax
import jax.numpy as jnp
from jax import lax
from jax.experimental import pallas as pl
from jax.experimental.pallas import tpu as pltpu
from jax.sharding import PartitionSpec as P

NB = 128
SUB = 8
CW = 256
TILE = 256
MESH = pl.DeviceIdType.MESH
f32 = jnp.float32
bf16 = jnp.bfloat16


def dot(a, b, ca=1, cb=0):
    return lax.dot_general(
        a,
        b,
        (((ca,), (cb,)), ((), ())),
        precision=lax.Precision.HIGHEST,
        preferred_element_type=f32,
    )


def split(x):
    h = x.astype(bf16).astype(f32)
    rest = x - h
    m = rest.astype(bf16).astype(f32)
    return h, m, rest - m


def eliminate(aug, steps):
    row = lax.broadcasted_iota(jnp.int32, (SUB, 2 * NB), 0)
    for b in range(NB // SUB):
        lo = b * SUB
        block = aug[lo : lo + SUB, :]
        rows = [jnp.broadcast_to(block[k : k + 1, :], (SUB, 2 * NB)) for k in range(SUB)]
        d = {}
        for k in range(SUB):
            for j in range(k, SUB):
                d[k, j] = jnp.broadcast_to(rows[k][:, lo + j : lo + j + 1], (SUB, NB))
        for j in range(SUB):
            inv = lax.rsqrt(d[j, j])
            rows[j] = rows[j] * jnp.concatenate([inv, inv], axis=1)
            for i in range(j + 1, SUB):
                d[j, i] = d[j, i] * inv
            for i in range(j + 1, SUB):
                m = d[j, i]
                for l in range(i, SUB):
                    d[i, l] = d[i, l] - m * d[j, l]
                rows[i] = rows[i] - jnp.concatenate([m, m], axis=1) * rows[j]
        u = rows[0]
        for k in range(1, SUB):
            u = jnp.where(row == k, rows[k], u)
        aug[lo : lo + SUB, :] = u
        if lo + SUB < NB:
            h, m, l = split(u)
            left = jnp.concatenate([h, h, m, h, m, l], axis=0)[:, :NB].T[lo + SUB :, :]
            right = jnp.concatenate([h, m, h, l, m, h], axis=0)
            aug[lo + SUB :, :] = aug[lo + SUB :, :] - jnp.dot(
                left.astype(bf16), right.astype(bf16), preferred_element_type=f32
            )
        for step in steps.pop(0) if steps else ():
            step()


def panels_kernel(
    nrow, ncol, rows_here, cols_here,
    a, r_out, c_out,
    p, ac, k, aug, low, fac,
    psend, precv, zsend, ksend, ksib, krecv, asend, arecv, loc,
):
    chips = nrow // 2
    nx = math.isqrt(chips)
    ny = chips // nx
    nt = rows_here // NB
    na = cols_here // CW
    r = lax.axis_index("row")
    c = lax.axis_index("col")
    core = lax.rem(r, 2)
    q = r // 2
    qx = lax.rem(q, nx)
    qy = q // nx
    sib = r + 1 - 2 * core
    first = core == 0

    barrier = pltpu.get_barrier_semaphore()
    for i in range(1, ncol):
        pl.semaphore_signal(barrier, inc=1, device_id=(r, lax.rem(c + i, ncol)), device_id_type=MESH)
    for i in range(1, chips):
        pl.semaphore_signal(
            barrier, inc=1, device_id=(lax.rem(q + i, chips) * 2 + core, c), device_id_type=MESH
        )
    pl.semaphore_signal(barrier, inc=1, device_id=(sib, c), device_id_type=MESH)
    pl.semaphore_wait(barrier, ncol - 1 + chips)

    started = []

    def send(cond, src, dst, ss, rs, dev):
        def make():
            return pltpu.make_async_remote_copy(
                src_ref=src, dst_ref=dst, send_sem=ss, recv_sem=rs, device_id=dev, device_id_type=MESH
            )

        @pl.when(cond)
        def _():
            make().start()

        started.append((cond, make))

    def received(cond, dst, rs):
        @pl.when(cond)
        def _():
            pltpu.make_async_remote_copy(
                src_ref=dst, dst_ref=dst, send_sem=loc.at[3], recv_sem=rs,
                device_id=(sib, c), device_id_type=MESH,
            ).wait_recv()

    def pc(s, t):
        return p.at[s, pl.ds(t * NB, NB)]

    def ach(s, t):
        return ac.at[s, :, pl.ds(t * CW, CW)]

    def a_rows(t):
        return a.at[pl.ds(t * NB, NB), pl.ds(0, NB)]

    def own(i):
        if i == 0:
            return c == 0, pltpu.make_async_copy(a.at[:, pl.ds(0, NB)], p.at[0], loc.at[0])
        if i == 1:
            return c == 1, pltpu.make_async_copy(a.at[:, pl.ds(0, NB)], p.at[1], loc.at[1])
        return None

    for z in range(ncol - 1, 0, -1):
        send((r == 0) & (c == 0), a_rows(0), pc(0, 0), zsend.at[z], precv.at[0, 0], (r, z))

    def spread(s, cond, src):
        base = 0 if s == 0 else 1
        for j in range(chips - 1, 0, -1):
            send(cond, src, k.at[s], ksend.at[s, j], krecv.at[s], (2 * j + base, c))
        send(cond, src, k.at[s], ksib.at[s], krecv.at[s], (sib, c))

    for i in range(2):
        cond, copy = own(i)
        pl.when(cond)(copy.start)
    for s in range(2):
        @pl.when(r == s)
        def _():
            pltpu.make_async_copy(a.at[pl.ds(0, NB), :], ac.at[s], loc.at[2]).start()

    def p_source(t):
        first_sent = (c == 0) & (r != 0) if t == 0 else c == 0
        send(first_sent, a_rows(t), pc(0, t), psend.at[0, t, 0], precv.at[0, t], (r, 1))
        send(c == 1, a_rows(t), pc(1, t), psend.at[1, t, 0], precv.at[1, t], (r, 0))
        if ncol > 2:
            send(c == 1, a_rows(t), pc(1, t), psend.at[1, t, 1], precv.at[1, t], (r, 2))

    p_source(0)
    received((r == 0) & (c != 0), pc(0, 0), precv.at[0, 0])
    for i in range(2):
        cond, copy = own(i)
        pl.when(cond)(copy.wait)
    spread(0, r == 0, pc(0, 0))

    def a_children(cond, s, t, src, base):
        down = (qy < ny - 1) if s else (qy < ny - 1) & (qx == 0)
        over = (qx < nx - 1) & (qy == 0) if s else (qx < nx - 1)
        send(cond & over, src, ach(s, t), asend.at[s, t, 0], arecv.at[s, t], (r + 2, c))
        send(cond & down, src, ach(s, t), asend.at[s, t, 1], arecv.at[s, t], (r + 2 * nx, c))
        send(cond, src, ach(s, t), asend.at[s, t, 2], arecv.at[s, t], (sib, c))

    def a_source(t):
        for s in range(2):
            a_children(r == s, s, t, a.at[pl.ds(0, NB), pl.ds(t * CW, CW)], s)

    for t in range(1, nt):
        p_source(t)
    for t in range(na):
        a_source(t)

    received((q != 0) & first, k.at[0], krecv.at[0])
    send((q != 0) & first, k.at[0], k.at[0], ksib.at[0], krecv.at[0], (sib, c))
    received(core == 1, k.at[0], krecv.at[0])

    def p_pass(t):
        if t == 0:
            received((c != 0) & (r != 0), pc(0, 0), precv.at[0, 0])
            received(c != 1, pc(1, 0), precv.at[1, 0])
        else:
            received((c > 0) & (c < ncol - 1), pc(0, t), precv.at[0, t])
            received((c > 1) & (c < ncol - 1), pc(1, t), precv.at[1, t])
        go = (c > 0) & (c < ncol - 1)
        send(go & (r != 0) if t == 0 else go, pc(0, t), pc(0, t), psend.at[0, t, 0], precv.at[0, t], (r, c + 1))
        send((c > 1) & (c < ncol - 1), pc(1, t), pc(1, t), psend.at[1, t, 0], precv.at[1, t], (r, c + 1))

    def k_first():
        spread(1, r == 1, pc(0, 0))
        spread(2, r == 1, pc(1, 0))

    def k_pass():
        for s in (1, 2):
            cond = (core == 1) & (q != 0)
            received(cond, k.at[s], krecv.at[s])
            send(cond, k.at[s], k.at[s], ksib.at[s], krecv.at[s], (sib, c))

    def a_pass(t):
        for s in range(2):
            cond = (q != 0) & (core == s)
            received(cond, ach(s, t), arecv.at[s, t])
            a_children(cond, s, t, ach(s, t), s)

    items = [functools.partial(p_pass, 0), k_first, functools.partial(a_pass, 0), k_pass]
    for t in range(1, max(nt, na)):
        if t < nt:
            items.append(functools.partial(p_pass, t))
        if t < na:
            items.append(functools.partial(a_pass, t))
    half = NB // SUB
    places = [[] for _ in range(2 * half)]
    for n, item in enumerate(items):
        places[min(1 + 2 * n, 2 * half - 1)].append(item)
    for n in range(4):
        if items[n] not in sum(places[:half], []):
            raise ValueError("order")

    eye = jnp.where(
        lax.broadcasted_iota(jnp.int32, (NB, NB), 0) == lax.broadcasted_iota(jnp.int32, (NB, NB), 1),
        f32(1.0), f32(0.0),
    )

    @pl.when(r == 0)
    def _():
        aug[0, :, :NB] = p[0, :NB, :]

    @pl.when(r != 0)
    def _():
        aug[0, :, :NB] = k[0]

    aug[0, :, NB:] = eye
    eliminate(aug.at[0], places[:half])

    received(first, k.at[1], krecv.at[1])
    received(first, k.at[2], krecv.at[2])

    @pl.when(r == 1)
    def _():
        k[1] = p[0, :NB, :]
        k[2] = p[1, :NB, :]

    w0 = aug[0, :, NB:]
    low[...] = dot(k[1], w0, 1, 1)
    l10 = low[...]
    aug[1, :, :NB] = k[2] - dot(l10, l10, 1, 1)
    aug[1, :, NB:] = eye
    eliminate(aug.at[1], places[half:])

    upper = lax.broadcasted_iota(jnp.int32, (NB, NB), 0) <= lax.broadcasted_iota(jnp.int32, (NB, NB), 1)
    fac[0] = jnp.where(upper, aug[0, :, :NB], f32(0.0)).T
    fac[1] = jnp.where(upper, aug[1, :, :NB], f32(0.0)).T

    for t in range(1, nt):
        received(c == ncol - 1, pc(0, t), precv.at[0, t])
        received((c == 0) | ((c == ncol - 1) & (c != 1)), pc(1, t), precv.at[1, t])
    for s in range(2):
        @pl.when(r == s)
        def _():
            pltpu.make_async_copy(a.at[pl.ds(0, NB), :], ac.at[s], loc.at[2]).wait()

    for t in range(nt):
        here = slice(t * NB, (t + 1) * NB)
        p0 = dot(p[0, here, :], aug[0, :, NB:], 1, 1)
        p1 = dot(p[1, here, :] - dot(p0, low[...], 1, 1), aug[1, :, NB:], 1, 1)
        r_out[here, :NB] = p0
        r_out[here, NB:] = p1

    @pl.when(r == 0)
    def _():
        r_out[:NB, :NB] = fac[0]
        r_out[:NB, NB:] = jnp.zeros((NB, NB), f32)

    @pl.when(r == 1)
    def _():
        r_out[:NB, NB:] = fac[1]

    for t in range(na):
        received(first, ach(1, t), arecv.at[1, t])
        received(core == 1, ach(0, t), arecv.at[0, t])
        here = slice(t * CW, (t + 1) * CW)
        c0 = dot(aug[0, :, NB:], ac[0, :, here])
        c1 = dot(aug[1, :, NB:], ac[1, :, here] - dot(low[...], c0))
        c_out[:NB, here] = c0
        c_out[NB:, here] = c1

    for cond, make in started:
        @pl.when(cond)
        def _():
            make().wait_send()


def update_kernel(a, left, right, out, parts):
    r = lax.axis_index("row")
    c = lax.axis_index("col")
    j = pl.program_id(0)

    @pl.when(j == 0)
    def _():
        x = left[...]
        h = x.astype(bf16)
        parts[0] = h
        parts[1] = (x - h.astype(f32)).astype(bf16)

    y = right[...]
    yh = y.astype(bf16)
    yl = (y - yh.astype(f32)).astype(bf16)
    mm = functools.partial(jnp.dot, preferred_element_type=f32)
    out[...] = a[...] - (mm(parts[0], yh) + (mm(parts[0], yl) + mm(parts[1], yh)))

    @pl.when(r < 2)
    def _():
        out[:NB, :] = jnp.zeros((NB, out.shape[1]), f32)

    for s in range(2):
        @pl.when((j == 0) & (c == s))
        def _():
            out[:, :NB] = left[:, s * NB : (s + 1) * NB]


def local(nrow, ncol, kernel):
    rows, cols = kernel.shape
    nt = rows // NB
    na = cols // CW
    chips = nrow // 2
    dma = pltpu.SemaphoreType.DMA
    left, right = pl.pallas_call(
        functools.partial(panels_kernel, nrow, ncol, rows, cols),
        out_shape=[
            jax.ShapeDtypeStruct((rows, 2 * NB), f32),
            jax.ShapeDtypeStruct((2 * NB, cols), f32),
        ],
        in_specs=[pl.BlockSpec(memory_space=pl.ANY)],
        out_specs=[pl.BlockSpec(memory_space=pltpu.VMEM)] * 2,
        scratch_shapes=[
            pltpu.VMEM((2, rows, NB), f32),
            pltpu.VMEM((2, NB, cols), f32),
            pltpu.VMEM((3, NB, NB), f32),
            pltpu.VMEM((2, NB, 2 * NB), f32),
            pltpu.VMEM((NB, NB), f32),
            pltpu.VMEM((2, NB, NB), f32),
            dma((2, nt, 2)),
            dma((2, nt)),
            dma((ncol,)),
            dma((3, chips)),
            dma((3,)),
            dma((3,)),
            dma((2, na, 3)),
            dma((2, na)),
            dma((4,)),
        ],
        compiler_params=pltpu.CompilerParams(
            collective_id=0, has_side_effects=True, vmem_limit_bytes=48 * 1024 * 1024
        ),
        name="panels",
    )(kernel)
    return pl.pallas_call(
        update_kernel,
        out_shape=jax.ShapeDtypeStruct((rows, cols), f32),
        grid=(cols // TILE,),
        in_specs=[
            pl.BlockSpec((rows, TILE), lambda j: (0, j)),
            pl.BlockSpec((rows, 2 * NB), lambda j: (0, 0)),
            pl.BlockSpec((2 * NB, TILE), lambda j: (0, j)),
        ],
        out_specs=pl.BlockSpec((rows, TILE), lambda j: (0, j)),
        scratch_shapes=[pltpu.VMEM((2, rows, 2 * NB), bf16)],
        compiler_params=pltpu.CompilerParams(vmem_limit_bytes=32 * 1024 * 1024),
        name="update",
    )(kernel, left, right)


def solution(mesh):
    return jax.shard_map(
        functools.partial(local, mesh.shape["row"], mesh.shape["col"]),
        mesh=mesh,
        in_specs=(P("row", "col"),),
        out_specs=P("row", "col"),
        check_vma=False,
    )
```

time: 344 us -> 52.7 us (0.15)
  the two profiles are of different devices: /device:TPU:20 before, /device:TPU:31 now
where the time goes in v1:
time: 52.7 us; the launch traced here: 52.5 us
  Pallas kernels  50.6 us (96%)
  local copies, waits for them, and re-layouts  1.93 us (4%)
    pallas_call x1, Pallas kernels, local(): pl.pallas_call(functools.partial(panels_kernel, nrow, ncol, rows, cols),...  46.4 us
    pallas_call x1, Pallas kernels, local(): pl.pallas_call(update_kernel, out_shape=jax.ShapeDtypeStruct((rows, cols)...  4.16 us
    unnamed x2, local copies, waits for them, and re-layouts  1.93 us

profile of v1, /device:TPU:31, one launch (start us, length us, event | category | flops | bytes accessed | tf_op | source)
XLA Modules:
  0.0 52.5 jit_solution(15677617743942523349)
XLA Ops:
  0.0 0.0 copy-start
  0.0 1.9 %copy-done = f32[640,1280]{1,0:T(8,128)S(1)} copy-done((f32[640,1280]{1,0:T(8,128)S(1)}, f32[640,1280]{1,0:T(8,128)}, u32[]{:S(2)}) %copy-start) | copy-done | bytes 3276824
  1.9 46.4 %panels.1 = (f32[640,256]{1,0:T(8,128)S(1)}, f32[256,1280]{1,0:T(8,128)S(1)}) custom-call(f32[640,1280]{1,0:T(8,128)S(1)} %copy-done), custom_call_target="tpu_custom_call" | custom-call | tf_op jit(solution)/shard_map/panels/pallas_call | solution.py:340
  48.4 4.2 %update.1 = f32[640,1280]{1,0:T(8,128)} custom-call(f32[640,1280]{1,0:T(8,128)S(1)} %copy-done, f32[640,256]{1,0:T(8,128)S(1)} %get-tuple-element.7.left, f32[256,1280]{1,0:T(8,128)S(1)} %get-tuple-element.8.right), custom_call_target="tpu_custom_call" | custom-call | tf_op jit(solution)/shard_map/update/pallas_call | solution.py:370
Async XLA Ops:
  0.0 1.9 %copy-start = (f32[640,1280]{1,0:T(8,128)S(1)}, f32[640,1280]{1,0:T(8,128)}, u32[]{:S(2)}) copy-start(f32[640,1280]{1,0:T(8,128)} %a.3) | copy-start | bytes 9830404

commit v2 on v1

--- a/solution.py
+++ b/solution.py
@@ -10,6 +10,7 @@
 
 NB = 128
 SUB = 8
+GROUP = 32
 CW = 256
 TILE = 256
 MESH = pl.DeviceIdType.MESH
@@ -34,45 +35,72 @@
     return h, m, rest - m
 
 
+def two(x):
+    h = x.astype(bf16)
+    return h, (x - h.astype(f32)).astype(bf16)
+
+
+def mm(a, b):
+    return jnp.dot(a, b, preferred_element_type=f32)
+
+
+def splat(x, lane):
+    return jnp.broadcast_to(x[:, lane : lane + 1], (SUB, NB))
+
+
 def eliminate(aug, steps):
-    row = lax.broadcasted_iota(jnp.int32, (SUB, 2 * NB), 0)
-    for b in range(NB // SUB):
-        lo = b * SUB
-        block = aug[lo : lo + SUB, :]
-        rows = [jnp.broadcast_to(block[k : k + 1, :], (SUB, 2 * NB)) for k in range(SUB)]
-        d = {}
-        for k in range(SUB):
-            for j in range(k, SUB):
-                d[k, j] = jnp.broadcast_to(rows[k][:, lo + j : lo + j + 1], (SUB, NB))
-        for j in range(SUB):
-            inv = lax.rsqrt(d[j, j])
-            rows[j] = rows[j] * jnp.concatenate([inv, inv], axis=1)
-            for i in range(j + 1, SUB):
-                d[j, i] = d[j, i] * inv
-            for i in range(j + 1, SUB):
-                m = d[j, i]
-                for l in range(i, SUB):
-                    d[i, l] = d[i, l] - m * d[j, l]
-                rows[i] = rows[i] - jnp.concatenate([m, m], axis=1) * rows[j]
-        u = rows[0]
-        for k in range(1, SUB):
-            u = jnp.where(row == k, rows[k], u)
-        aug[lo : lo + SUB, :] = u
-        if lo + SUB < NB:
+    row = lax.broadcasted_iota(jnp.int32, (SUB, NB), 0)
+    subs = GROUP // SUB
+    for g in range(NB // GROUP):
+        top = g * GROUP
+        rows = [
+            [[jnp.broadcast_to(block[k : k + 1, h * NB : (h + 1) * NB], (SUB, NB)) for h in range(2)] for k in range(SUB)]
+            for block in (aug[top + s * SUB : top + (s + 1) * SUB, :] for s in range(subs))
+        ]
+        done = []
+        for s in range(subs):
+            lo = top + s * SUB
+            mine = rows[s]
+            wide = 2 * SUB if s + 1 < subs else SUB
+            d = {(k, j): splat(mine[k][0], lo + j) for k in range(SUB) for j in range(k, wide)}
+            for j in range(SUB):
+                inv = lax.rsqrt(d[j, j])
+                for i in range(j + 1, wide):
+                    d[j, i] = d[j, i] * inv
+                for i in range(j + 1, SUB):
+                    for l in range(i, wide):
+                        d[i, l] = d[i, l] - d[j, i] * d[j, l]
+                mine[j] = [x * inv for x in mine[j]]
+                for i in range(j + 1, SUB):
+                    mine[i] = [x - d[j, i] * y for x, y in zip(mine[i], mine[j])]
+            for later in range(s + 1, subs):
+                for i in range(SUB):
+                    for k in range(SUB):
+                        m = d[k, SUB + i] if later == s + 1 else splat(mine[k][0], top + later * SUB + i)
+                        rows[later][i] = [x - m * y for x, y in zip(rows[later][i], mine[k])]
+            halves = []
+            for h in range(2):
+                u = mine[0][h]
+                for k in range(1, SUB):
+                    u = jnp.where(row == k, mine[k][h], u)
+                halves.append(u)
+            done.append(jnp.concatenate(halves, axis=1))
+        u = jnp.concatenate(done, axis=0)
+        aug[top : top + GROUP, :] = u
+        if top + GROUP < NB:
             h, m, l = split(u)
-            left = jnp.concatenate([h, h, m, h, m, l], axis=0)[:, :NB].T[lo + SUB :, :]
-            right = jnp.concatenate([h, m, h, l, m, h], axis=0)
-            aug[lo + SUB :, :] = aug[lo + SUB :, :] - jnp.dot(
-                left.astype(bf16), right.astype(bf16), preferred_element_type=f32
-            )
+            left = jnp.concatenate([h, h, m, h, m, l], axis=0)[:, :NB].astype(bf16)
+            right = jnp.concatenate([h, m, h, l, m, h], axis=0).astype(bf16)
+            taken = lax.dot_general(left, right, (((0,), (0,)), ((), ())), preferred_element_type=f32)
+            aug[top + GROUP :, :] = aug[top + GROUP :, :] - taken[top + GROUP :, :]
         for step in steps.pop(0) if steps else ():
             step()
 
 
 def panels_kernel(
     nrow, ncol, rows_here, cols_here,
-    a, r_out, c_out,
-    p, ac, k, aug, low, fac,
+    a, panel, left, right,
+    p, ac, k, aug, low,
     psend, precv, zsend, ksend, ksib, krecv, asend, arecv, loc,
 ):
     chips = nrow // 2
@@ -154,14 +182,14 @@
         def _():
             pltpu.make_async_copy(a.at[pl.ds(0, NB), :], ac.at[s], loc.at[2]).start()
 
-    def p_source(t):
-        first_sent = (c == 0) & (r != 0) if t == 0 else c == 0
-        send(first_sent, a_rows(t), pc(0, t), psend.at[0, t, 0], precv.at[0, t], (r, 1))
-        send(c == 1, a_rows(t), pc(1, t), psend.at[1, t, 0], precv.at[1, t], (r, 0))
+    def p_source(t, here):
+        zero = here & (c == 0) & (r != 0) if t == 0 else here & (c == 0)
+        one = here & (c == 1)
+        send(zero, a_rows(t), pc(0, t), psend.at[0, t, 0], precv.at[0, t], (r, 1))
+        send(one, a_rows(t), pc(1, t), psend.at[1, t, 0], precv.at[1, t], (r, 0))
         if ncol > 2:
-            send(c == 1, a_rows(t), pc(1, t), psend.at[1, t, 1], precv.at[1, t], (r, 2))
-
-    p_source(0)
+            send(one, a_rows(t), pc(1, t), psend.at[1, t, 1], precv.at[1, t], (r, 2))
+
     received((r == 0) & (c != 0), pc(0, 0), precv.at[0, 0])
     for i in range(2):
         cond, copy = own(i)
@@ -179,10 +207,8 @@
         for s in range(2):
             a_children(r == s, s, t, a.at[pl.ds(0, NB), pl.ds(t * CW, CW)], s)
 
-    for t in range(1, nt):
-        p_source(t)
-    for t in range(na):
-        a_source(t)
+    for t in range(nt):
+        p_source(t, q != 0)
 
     received((q != 0) & first, k.at[0], krecv.at[0])
     send((q != 0) & first, k.at[0], k.at[0], ksib.at[0], krecv.at[0], (sib, c))
@@ -215,19 +241,19 @@
             received(cond, ach(s, t), arecv.at[s, t])
             a_children(cond, s, t, ach(s, t), s)
 
-    items = [functools.partial(p_pass, 0), k_first, functools.partial(a_pass, 0), k_pass]
-    for t in range(1, max(nt, na)):
-        if t < nt:
-            items.append(functools.partial(p_pass, t))
+    half = NB // GROUP
+    places = [[] for _ in range(2 * half)]
+    places[0] += [functools.partial(p_source, 0, q == 0)]
+    places[0] += [functools.partial(p_pass, 0), k_first]
+    places[0] += [functools.partial(p_source, t, q == 0) for t in range(1, nt)]
+    places[1] += [functools.partial(a_source, t) for t in range(na)]
+    places[2] += [k_pass]
+    for t in range(max(nt, na)):
+        at = places[min(3 + t, 2 * half - 1)]
+        if 1 <= t < nt:
+            at.append(functools.partial(p_pass, t))
         if t < na:
-            items.append(functools.partial(a_pass, t))
-    half = NB // SUB
-    places = [[] for _ in range(2 * half)]
-    for n, item in enumerate(items):
-        places[min(1 + 2 * n, 2 * half - 1)].append(item)
-    for n in range(4):
-        if items[n] not in sum(places[:half], []):
-            raise ValueError("order")
+            at.append(functools.partial(a_pass, t))
 
     eye = jnp.where(
         lax.broadcasted_iota(jnp.int32, (NB, NB), 0) == lax.broadcasted_iota(jnp.int32, (NB, NB), 1),
@@ -260,9 +286,15 @@
     aug[1, :, NB:] = eye
     eliminate(aug.at[1], places[half:])
 
-    upper = lax.broadcasted_iota(jnp.int32, (NB, NB), 0) <= lax.broadcasted_iota(jnp.int32, (NB, NB), 1)
-    fac[0] = jnp.where(upper, aug[0, :, :NB], f32(0.0)).T
-    fac[1] = jnp.where(upper, aug[1, :, :NB], f32(0.0)).T
+    w1 = aug[1, :, NB:]
+    w10 = -dot(w1, dot(l10, w0))
+    w = jnp.concatenate(
+        [jnp.concatenate([w0, jnp.zeros((NB, NB), f32)], axis=1), jnp.concatenate([w10, w1], axis=1)], axis=0
+    )
+    wh, wl = two(w)
+    w_left = jnp.concatenate([wh, wl, wh], axis=1)
+    wh, wl = two(w.T)
+    w_right = jnp.concatenate([wh, wh, wl], axis=0)
 
     for t in range(1, nt):
         received(c == ncol - 1, pc(0, t), precv.at[0, t])
@@ -272,30 +304,33 @@
         def _():
             pltpu.make_async_copy(a.at[pl.ds(0, NB), :], ac.at[s], loc.at[2]).wait()
 
-    for t in range(nt):
-        here = slice(t * NB, (t + 1) * NB)
-        p0 = dot(p[0, here, :], aug[0, :, NB:], 1, 1)
-        p1 = dot(p[1, here, :] - dot(p0, low[...], 1, 1), aug[1, :, NB:], 1, 1)
-        r_out[here, :NB] = p0
-        r_out[here, NB:] = p1
+    rh0, rl0 = two(p[0])
+    rh1, rl1 = two(p[1])
+    rows = mm(jnp.concatenate([rh0, rh1, rl0, rl1, rh0, rh1], axis=1), w_right)
+    panel[...] = rows
+    rh, rl = two(rows)
+    left[...] = jnp.concatenate([rh, rl, rh], axis=1)
+
+    upper = lax.broadcasted_iota(jnp.int32, (NB, NB), 0) <= lax.broadcasted_iota(jnp.int32, (NB, NB), 1)
 
     @pl.when(r == 0)
     def _():
-        r_out[:NB, :NB] = fac[0]
-        r_out[:NB, NB:] = jnp.zeros((NB, NB), f32)
+        panel[:NB, :NB] = jnp.where(upper, aug[0, :, :NB], f32(0.0)).T
+        panel[:NB, NB:] = jnp.zeros((NB, NB), f32)
 
     @pl.when(r == 1)
     def _():
-        r_out[:NB, NB:] = fac[1]
+        panel[:NB, NB:] = jnp.where(upper, aug[1, :, :NB], f32(0.0)).T
 
     for t in range(na):
         received(first, ach(1, t), arecv.at[1, t])
         received(core == 1, ach(0, t), arecv.at[0, t])
         here = slice(t * CW, (t + 1) * CW)
-        c0 = dot(aug[0, :, NB:], ac[0, :, here])
-        c1 = dot(aug[1, :, NB:], ac[1, :, here] - dot(low[...], c0))
-        c_out[:NB, here] = c0
-        c_out[NB:, here] = c1
+        h0, l0 = two(ac[0, :, here])
+        h1, l1 = two(ac[1, :, here])
+        cols = mm(w_left, jnp.concatenate([h0, h1, h0, h1, l0, l1], axis=0))
+        ch, cl = two(cols)
+        right[:, here] = jnp.concatenate([ch, ch, cl], axis=0)
 
     for cond, make in started:
         @pl.when(cond)
@@ -303,32 +338,29 @@
             make().wait_send()
 
 
-def update_kernel(a, left, right, out, parts):
+def update_kernel(a, panel, left, right, out, held, sems):
     r = lax.axis_index("row")
     c = lax.axis_index("col")
-    j = pl.program_id(0)
-
-    @pl.when(j == 0)
-    def _():
-        x = left[...]
-        h = x.astype(bf16)
-        parts[0] = h
-        parts[1] = (x - h.astype(f32)).astype(bf16)
-
-    y = right[...]
-    yh = y.astype(bf16)
-    yl = (y - yh.astype(f32)).astype(bf16)
-    mm = functools.partial(jnp.dot, preferred_element_type=f32)
-    out[...] = a[...] - (mm(parts[0], yh) + (mm(parts[0], yl) + mm(parts[1], yh)))
-
-    @pl.when(r < 2)
-    def _():
-        out[:NB, :] = jnp.zeros((NB, out.shape[1]), f32)
-
-    for s in range(2):
-        @pl.when((j == 0) & (c == s))
-        def _():
-            out[:, :NB] = left[:, s * NB : (s + 1) * NB]
+    copies = []
+    for t in range(a.shape[1] // TILE):
+        here = pl.ds(t * TILE, TILE)
+        held[:, here] = a[:, here] - mm(left[...], right[:, here])
+
+        @pl.when(r < 2)
+        def _():
+            held[:NB, here] = jnp.zeros((NB, TILE), f32)
+
+        if t == 0:
+            for s in range(2):
+                @pl.when(c == s)
+                def _():
+                    held[:, :NB] = panel[:, s * NB : (s + 1) * NB]
+
+        copy = pltpu.make_async_copy(held.at[:, here], out.at[:, here], sems.at[t])
+        copy.start()
+        copies.append(copy)
+    for copy in copies:
+        copy.wait()
 
 
 def local(nrow, ncol, kernel):
@@ -337,21 +369,21 @@
     na = cols // CW
     chips = nrow // 2
     dma = pltpu.SemaphoreType.DMA
-    left, right = pl.pallas_call(
+    panel, left, right = pl.pallas_call(
         functools.partial(panels_kernel, nrow, ncol, rows, cols),
         out_shape=[
             jax.ShapeDtypeStruct((rows, 2 * NB), f32),
-            jax.ShapeDtypeStruct((2 * NB, cols), f32),
+            jax.ShapeDtypeStruct((rows, 6 * NB), bf16),
+            jax.ShapeDtypeStruct((6 * NB, cols), bf16),
         ],
-        in_specs=[pl.BlockSpec(memory_space=pl.ANY)],
-        out_specs=[pl.BlockSpec(memory_space=pltpu.VMEM)] * 2,
+        in_specs=[pl.BlockSpec(memory_space=pltpu.HBM)],
+        out_specs=[pl.BlockSpec(memory_space=pltpu.VMEM)] * 3,
         scratch_shapes=[
             pltpu.VMEM((2, rows, NB), f32),
             pltpu.VMEM((2, NB, cols), f32),
             pltpu.VMEM((3, NB, NB), f32),
             pltpu.VMEM((2, NB, 2 * NB), f32),
             pltpu.VMEM((NB, NB), f32),
-            pltpu.VMEM((2, NB, NB), f32),
             dma((2, nt, 2)),
             dma((2, nt)),
             dma((ncol,)),
@@ -370,17 +402,12 @@
     return pl.pallas_call(
         update_kernel,
         out_shape=jax.ShapeDtypeStruct((rows, cols), f32),
-        grid=(cols // TILE,),
-        in_specs=[
-            pl.BlockSpec((rows, TILE), lambda j: (0, j)),
-            pl.BlockSpec((rows, 2 * NB), lambda j: (0, 0)),
-            pl.BlockSpec((2 * NB, TILE), lambda j: (0, j)),
-        ],
-        out_specs=pl.BlockSpec((rows, TILE), lambda j: (0, j)),
-        scratch_shapes=[pltpu.VMEM((2, rows, 2 * NB), bf16)],
+        in_specs=[pl.BlockSpec(memory_space=pltpu.VMEM)] * 4,
+        out_specs=pl.BlockSpec(memory_space=pltpu.HBM),
+        scratch_shapes=[pltpu.VMEM((rows, cols), f32), pltpu.SemaphoreType.DMA((cols // TILE,))],
         compiler_params=pltpu.CompilerParams(vmem_limit_bytes=32 * 1024 * 1024),
         name="update",
-    )(kernel, left, right)
+    )(kernel, panel, left, right)
 
 
 def solution(mesh):

time: 52.7 us -> 47.1 us (0.89)
  Pallas kernels: 50.6 us -> 46.8 us
  local copies, waits for them, and re-layouts: 1.93 us -> 0.01 us
    pallas_call x1, Pallas kernels: 46.4 us -> 42.9 us  [local(): pl.pallas_call(functools.partial(panels_kernel, nrow, ncol, rows, cols),...]
    unnamed x2, local copies, waits for them, and re-layouts: 1.93 us -> 0.01 us
where the time goes in v2:
time: 47.1 us; the launch traced here: 47 us
  Pallas kernels  46.8 us (99%)
    pallas_call x1, Pallas kernels, local(): pl.pallas_call(functools.partial(panels_kernel, nrow, ncol, rows, cols),...  42.9 us
    pallas_call x1, Pallas kernels, local(): pl.pallas_call(update_kernel, out_shape=jax.ShapeDtypeStruct((rows, cols)...  3.94 us

profile of v2, /device:TPU:31, one launch (start us, length us, event | category | flops | bytes accessed | tf_op | source)
XLA Modules:
  0.0 47.0 jit_solution(18050375606715467639)
XLA Ops:
  0.0 0.0 copy-start
  0.0 42.9 %panels.1 = (f32[640,256]{1,0:T(8,128)S(1)}, bf16[640,768]{1,0:T(8,128)(2,1)S(1)}, bf16[768,1280]{1,0:T(8,128)(2,1)S(1)}) custom-call(f32[640,1280]{1,0:T(8,128)} %a.3), custom_call_target="tpu_custom_call" | custom-call | tf_op jit(solution)/shard_map/panels/pallas_call | solution.py:372
  42.9 0.0 copy-done
  42.9 3.9 %update.1 = f32[640,1280]{1,0:T(8,128)} custom-call(f32[640,1280]{1,0:T(8,128)S(1)} %copy-done, f32[640,256]{1,0:T(8,128)S(1)} %get-tuple-element.8.panel, bf16[640,768]{1,0:T(8,128)(2,1)S(1)} %get-tuple-element.9.left, bf16[768,1280]{1,0:T(8,128)(2,1)S(1)} %get-tuple-element.10.right), custom_call_target="tpu_custom_call" | custom-call | tf_op jit(solution)/shard_map/update/pallas_call | solution.py:402
Async XLA Ops:
  0.0 42.9 %copy-start = (f32[640,1280]{1,0:T(8,128)S(1)}, f32[640,1280]{1,0:T(8,128)}, u32[]{:S(2)}) copy-start(f32[640,1280]{1,0:T(8,128)} %a.3) | copy-start | bytes 9830404

commit v3 on v2

--- a/solution.py
+++ b/solution.py
@@ -85,6 +85,9 @@
                     u = jnp.where(row == k, mine[k][h], u)
                 halves.append(u)
             done.append(jnp.concatenate(halves, axis=1))
+            if s % 2 and s + 1 < subs:
+                for step in steps.pop(0):
+                    step()
         u = jnp.concatenate(done, axis=0)
         aug[top : top + GROUP, :] = u
         if top + GROUP < NB:
@@ -93,7 +96,7 @@
             right = jnp.concatenate([h, m, h, l, m, h], axis=0).astype(bf16)
             taken = lax.dot_general(left, right, (((0,), (0,)), ((), ())), preferred_element_type=f32)
             aug[top + GROUP :, :] = aug[top + GROUP :, :] - taken[top + GROUP :, :]
-        for step in steps.pop(0) if steps else ():
+        for step in steps.pop(0):
             step()
 
 
@@ -116,6 +119,21 @@
     qy = q // nx
     sib = r + 1 - 2 * core
     first = core == 0
+    second = core == 1
+    source = q == 0
+
+    oy = lax.rem(qy, 2)
+    ox = lax.rem(qx, 2)
+    if nx > 1 and ny > 1:
+        pos_x = qy * nx + qx + oy * (nx - 1 - 2 * qx)
+        pos_y = qx * ny + qy + ox * (ny - 1 - 2 * qy)
+        step_x = jnp.where(oy == 0, jnp.where(qx < nx - 1, 1, nx), jnp.where(qx > 0, -1, nx))
+        step_y = jnp.where(ox == 0, jnp.where(qy < ny - 1, nx, 1), jnp.where(qy > 0, -nx, 1))
+        pos = jnp.where(first, pos_x, pos_y)
+        onward = lax.rem(r + 2 * jnp.where(first, step_x, step_y) + nrow, nrow)
+    else:
+        pos = q
+        onward = lax.rem(r + 2, nrow)
 
     barrier = pltpu.get_barrier_semaphore()
     for i in range(1, ncol):
@@ -129,25 +147,28 @@
 
     started = []
 
-    def send(cond, src, dst, ss, rs, dev):
-        def make():
-            return pltpu.make_async_remote_copy(
-                src_ref=src, dst_ref=dst, send_sem=ss, recv_sem=rs, device_id=dev, device_id_type=MESH
-            )
-
+    def remote(src, dst, ss, rs, dev):
+        return functools.partial(
+            pltpu.make_async_remote_copy,
+            src_ref=src, dst_ref=dst, send_sem=ss, recv_sem=rs, device_id=dev, device_id_type=MESH,
+        )
+
+    def start(cond, *makes):
         @pl.when(cond)
         def _():
-            make().start()
-
-        started.append((cond, make))
-
-    def received(cond, dst, rs):
+            for make in makes:
+                make().start()
+
+        started.append((cond, makes))
+
+    def incoming(dst, rs):
+        return remote(dst, dst, loc.at[3], rs, (sib, c))
+
+    def received(cond, *makes):
         @pl.when(cond)
         def _():
-            pltpu.make_async_remote_copy(
-                src_ref=dst, dst_ref=dst, send_sem=loc.at[3], recv_sem=rs,
-                device_id=(sib, c), device_id_type=MESH,
-            ).wait_recv()
+            for make in makes:
+                make().wait_recv()
 
     def pc(s, t):
         return p.at[s, pl.ds(t * NB, NB)]
@@ -158,102 +179,112 @@
     def a_rows(t):
         return a.at[pl.ds(t * NB, NB), pl.ds(0, NB)]
 
-    def own(i):
-        if i == 0:
-            return c == 0, pltpu.make_async_copy(a.at[:, pl.ds(0, NB)], p.at[0], loc.at[0])
-        if i == 1:
-            return c == 1, pltpu.make_async_copy(a.at[:, pl.ds(0, NB)], p.at[1], loc.at[1])
-        return None
-
-    for z in range(ncol - 1, 0, -1):
-        send((r == 0) & (c == 0), a_rows(0), pc(0, 0), zsend.at[z], precv.at[0, 0], (r, z))
-
-    def spread(s, cond, src):
+    def p_in(s, t):
+        return incoming(pc(s, t), precv.at[s, t])
+
+    def p_copy(s, t, src, z, way=0):
+        return remote(src, pc(s, t), psend.at[s, t, way], precv.at[s, t], (r, z))
+
+    def direct(s):
+        return [
+            remote(a_rows(0), pc(s, 0), zsend.at[i], precv.at[s, 0], (r, z))
+            for i, z in enumerate([z for z in range(ncol - 1, -1, -1) if z != s])
+        ]
+
+    def spread(s, src):
         base = 0 if s == 0 else 1
-        for j in range(chips - 1, 0, -1):
-            send(cond, src, k.at[s], ksend.at[s, j], krecv.at[s], (2 * j + base, c))
-        send(cond, src, k.at[s], ksib.at[s], krecv.at[s], (sib, c))
-
-    for i in range(2):
-        cond, copy = own(i)
-        pl.when(cond)(copy.start)
+        return [
+            remote(src, k.at[s], ksend.at[s, j], krecv.at[s], (2 * j + base, c)) for j in range(chips - 1, 0, -1)
+        ] + [remote(src, k.at[s], ksib.at[s], krecv.at[s], (sib, c))]
+
+    def a_copies(t, src):
+        over = remote(src, ach(core, t), asend.at[t, 0], arecv.at[core, t], (onward, c))
+        across = remote(src, ach(core, t), asend.at[t, 1], arecv.at[core, t], (sib, c))
+        return over, across
+
+    def own(s):
+        return pltpu.make_async_copy(a.at[:, pl.ds(0, NB)], p.at[s], loc.at[s])
+
+    def own_slab():
+        return pltpu.make_async_copy(a.at[pl.ds(0, NB), :], ac.at[core], loc.at[2])
+
+    start((r == 0) & (c == 0), *direct(0))
     for s in range(2):
-        @pl.when(r == s)
-        def _():
-            pltpu.make_async_copy(a.at[pl.ds(0, NB), :], ac.at[s], loc.at[2]).start()
-
-    def p_source(t, here):
-        zero = here & (c == 0) & (r != 0) if t == 0 else here & (c == 0)
-        one = here & (c == 1)
-        send(zero, a_rows(t), pc(0, t), psend.at[0, t, 0], precv.at[0, t], (r, 1))
-        send(one, a_rows(t), pc(1, t), psend.at[1, t, 0], precv.at[1, t], (r, 0))
+        pl.when(c == s)(own(s).start)
+    rest = range(1, nt)
+
+    def p_source(here, ts):
+        start(here & (c == 0), *[p_copy(0, t, a_rows(t), 1) for t in ts])
+        start(
+            here & (c == 1),
+            *[p_copy(1, t, a_rows(t), z, i) for t in ts for i, z in enumerate((0, 2) if ncol > 2 else (0,))],
+        )
+
+    received((r == 0) & (c != 0), p_in(0, 0))
+    for s in range(2):
+        pl.when(c == s)(own(s).wait)
+    start(r == 0, *spread(0, pc(0, 0)))
+    pl.when(source)(lambda: own_slab().start())
+    p_source(q != 0, range(nt))
+    received((q != 0) & first, incoming(k.at[0], krecv.at[0]))
+    start((q != 0) & first, remote(k.at[0], k.at[0], ksib.at[0], krecv.at[0], (sib, c)))
+    received(second, incoming(k.at[0], krecv.at[0]))
+
+    def p_pass(t, z):
+        here = (c == 1) if z == 1 else (c > 1) & (c < ncol - 1)
+        if t == 0:
+            here = here & (q != 0)
+        panels = (0,) if z == 1 else (0, 1)
+        received(here, *[p_in(s, t) for s in panels])
+        start(here, *[p_copy(s, t, pc(s, t), c + 1) for s in panels])
+
+    def direct_rest():
+        start((r == 1) & (c == 0), *direct(0))
+        start(source & (c == 1), *direct(1))
+
+    def corner_rest():
+        received((r == 1) & (c != 0), p_in(0, 0))
+        received((r == 1) & (c != 1), p_in(1, 0))
+        start(r == 1, *spread(1, pc(0, 0)), *spread(2, pc(1, 0)))
+
+    def corner_pass():
+        here = second & (q != 0)
+        received(here, *[incoming(k.at[s], krecv.at[s]) for s in (1, 2)])
+        start(here, *[remote(k.at[s], k.at[s], ksib.at[s], krecv.at[s], (sib, c)) for s in (1, 2)])
+
+    def a_source():
+        makes = [a_copies(t, a.at[pl.ds(0, NB), pl.ds(t * CW, CW)]) for t in range(na)]
+        start(source, *[make for pair in makes for make in pair])
+
+    def a_pass(t, at):
+        here = pos == at if at < 3 else pos >= at
+        over, across = a_copies(t, ach(core, t))
+        received(here, incoming(ach(core, t), arecv.at[core, t]))
+        if at < 3:
+            start(here, over, across)
+        else:
+            start(here & (pos < chips - 1), over)
+            start(here, across)
+
+    half = NB // (2 * SUB)
+    places = [[] for _ in range(2 * half)]
+
+    def put(at, *step):
+        places[min(int(at), 2 * half - 1)].append(functools.partial(*step))
+
+    put(0, direct_rest)
+    put(1, p_source, source, rest)
+    put(1, a_source)
+    put(2, corner_rest)
+    put(5, corner_pass)
+    for t in range(nt):
         if ncol > 2:
-            send(one, a_rows(t), pc(1, t), psend.at[1, t, 1], precv.at[1, t], (r, 2))
-
-    received((r == 0) & (c != 0), pc(0, 0), precv.at[0, 0])
-    for i in range(2):
-        cond, copy = own(i)
-        pl.when(cond)(copy.wait)
-    spread(0, r == 0, pc(0, 0))
-
-    def a_children(cond, s, t, src, base):
-        down = (qy < ny - 1) if s else (qy < ny - 1) & (qx == 0)
-        over = (qx < nx - 1) & (qy == 0) if s else (qx < nx - 1)
-        send(cond & over, src, ach(s, t), asend.at[s, t, 0], arecv.at[s, t], (r + 2, c))
-        send(cond & down, src, ach(s, t), asend.at[s, t, 1], arecv.at[s, t], (r + 2 * nx, c))
-        send(cond, src, ach(s, t), asend.at[s, t, 2], arecv.at[s, t], (sib, c))
-
-    def a_source(t):
-        for s in range(2):
-            a_children(r == s, s, t, a.at[pl.ds(0, NB), pl.ds(t * CW, CW)], s)
-
-    for t in range(nt):
-        p_source(t, q != 0)
-
-    received((q != 0) & first, k.at[0], krecv.at[0])
-    send((q != 0) & first, k.at[0], k.at[0], ksib.at[0], krecv.at[0], (sib, c))
-    received(core == 1, k.at[0], krecv.at[0])
-
-    def p_pass(t):
-        if t == 0:
-            received((c != 0) & (r != 0), pc(0, 0), precv.at[0, 0])
-            received(c != 1, pc(1, 0), precv.at[1, 0])
-        else:
-            received((c > 0) & (c < ncol - 1), pc(0, t), precv.at[0, t])
-            received((c > 1) & (c < ncol - 1), pc(1, t), precv.at[1, t])
-        go = (c > 0) & (c < ncol - 1)
-        send(go & (r != 0) if t == 0 else go, pc(0, t), pc(0, t), psend.at[0, t, 0], precv.at[0, t], (r, c + 1))
-        send((c > 1) & (c < ncol - 1), pc(1, t), pc(1, t), psend.at[1, t, 0], precv.at[1, t], (r, c + 1))
-
-    def k_first():
-        spread(1, r == 1, pc(0, 0))
-        spread(2, r == 1, pc(1, 0))
-
-    def k_pass():
-        for s in (1, 2):
-            cond = (core == 1) & (q != 0)
-            received(cond, k.at[s], krecv.at[s])
-            send(cond, k.at[s], k.at[s], ksib.at[s], krecv.at[s], (sib, c))
-
-    def a_pass(t):
-        for s in range(2):
-            cond = (q != 0) & (core == s)
-            received(cond, ach(s, t), arecv.at[s, t])
-            a_children(cond, s, t, ach(s, t), s)
-
-    half = NB // GROUP
-    places = [[] for _ in range(2 * half)]
-    places[0] += [functools.partial(p_source, 0, q == 0)]
-    places[0] += [functools.partial(p_pass, 0), k_first]
-    places[0] += [functools.partial(p_source, t, q == 0) for t in range(1, nt)]
-    places[1] += [functools.partial(a_source, t) for t in range(na)]
-    places[2] += [k_pass]
-    for t in range(max(nt, na)):
-        at = places[min(3 + t, 2 * half - 1)]
-        if 1 <= t < nt:
-            at.append(functools.partial(p_pass, t))
-        if t < na:
-            at.append(functools.partial(a_pass, t))
+            put(1 + 2 * t, p_pass, t, 1)
+        if ncol > 3:
+            put(2 + 2 * t, p_pass, t, 2)
+    for t in range(na):
+        for at in range(1, min(chips, 4)):
+            put(2 + 1.5 * t + 2 * (at - 1), a_pass, t, at)
 
     eye = jnp.where(
         lax.broadcasted_iota(jnp.int32, (NB, NB), 0) == lax.broadcasted_iota(jnp.int32, (NB, NB), 1),
@@ -271,8 +302,7 @@
     aug[0, :, NB:] = eye
     eliminate(aug.at[0], places[:half])
 
-    received(first, k.at[1], krecv.at[1])
-    received(first, k.at[2], krecv.at[2])
+    received(first, *[incoming(k.at[s], krecv.at[s]) for s in (1, 2)])
 
     @pl.when(r == 1)
     def _():
@@ -296,13 +326,13 @@
     wh, wl = two(w.T)
     w_right = jnp.concatenate([wh, wh, wl], axis=0)
 
-    for t in range(1, nt):
-        received(c == ncol - 1, pc(0, t), precv.at[0, t])
-        received((c == 0) | ((c == ncol - 1) & (c != 1)), pc(1, t), precv.at[1, t])
-    for s in range(2):
-        @pl.when(r == s)
-        def _():
-            pltpu.make_async_copy(a.at[pl.ds(0, NB), :], ac.at[s], loc.at[2]).wait()
+    last = c == ncol - 1
+    received(last & (c > 0), *[p_in(0, t) for t in rest])
+    received((c == 0) | (last & (c > 1)), *[p_in(1, t) for t in rest])
+    received((q != 0) & last, p_in(0, 0))
+    received((q != 0) & ((c == 0) | (last & (c > 1))), p_in(1, 0))
+    received((r == 0) & (c != 1), p_in(1, 0))
+    pl.when(source)(lambda: own_slab().wait())
 
     rh0, rl0 = two(p[0])
     rh1, rl1 = two(p[1])
@@ -323,8 +353,7 @@
         panel[:NB, NB:] = jnp.where(upper, aug[1, :, :NB], f32(0.0)).T
 
     for t in range(na):
-        received(first, ach(1, t), arecv.at[1, t])
-        received(core == 1, ach(0, t), arecv.at[0, t])
+        incoming(ach(1 - core, t), arecv.at[1 - core, t])().wait_recv()
         here = slice(t * CW, (t + 1) * CW)
         h0, l0 = two(ac[0, :, here])
         h1, l1 = two(ac[1, :, here])
@@ -332,10 +361,11 @@
         ch, cl = two(cols)
         right[:, here] = jnp.concatenate([ch, ch, cl], axis=0)
 
-    for cond, make in started:
+    for cond, makes in started:
         @pl.when(cond)
         def _():
-            make().wait_send()
+            for make in makes:
+                make().wait_send()
 
 
 def update_kernel(a, panel, left, right, out, held, sems):
@@ -390,7 +420,7 @@
             dma((3, chips)),
             dma((3,)),
             dma((3,)),
-            dma((2, na, 3)),
+            dma((na, 2)),
             dma((2, na)),
             dma((4,)),
         ],

time: 47.1 us -> 41.3 us (0.88)
  the two profiles are of different devices: /device:TPU:31 before, /device:TPU:20 now
where the time goes in v3:
time: 41.3 us; the launch traced here: 41.1 us
  Pallas kernels  40.9 us (99%)
    pallas_call x1, Pallas kernels, local(): pl.pallas_call(functools.partial(panels_kernel, nrow, ncol, rows, cols),...  37 us
    pallas_call x1, Pallas kernels, local(): pl.pallas_call(update_kernel, out_shape=jax.ShapeDtypeStruct((rows, cols)...  3.94 us

profile of v3, /device:TPU:20, one launch (start us, length us, event | category | flops | bytes accessed | tf_op | source)
XLA Modules:
  0.0 41.1 jit_solution(14168140738342690622)
XLA Ops:
  0.0 0.0 copy-start
  0.0 37.0 %panels.1 = (f32[640,256]{1,0:T(8,128)S(1)}, bf16[640,768]{1,0:T(8,128)(2,1)S(1)}, bf16[768,1280]{1,0:T(8,128)(2,1)S(1)}) custom-call(f32[640,1280]{1,0:T(8,128)} %a.3), custom_call_target="tpu_custom_call" | custom-call | tf_op jit(solution)/shard_map/panels/pallas_call | solution.py:402
  37.0 0.0 copy-done
  37.0 3.9 %update.1 = f32[640,1280]{1,0:T(8,128)} custom-call(f32[640,1280]{1,0:T(8,128)S(1)} %copy-done, f32[640,256]{1,0:T(8,128)S(1)} %get-tuple-element.8.panel, bf16[640,768]{1,0:T(8,128)(2,1)S(1)} %get-tuple-element.9.left, bf16[768,1280]{1,0:T(8,128)(2,1)S(1)} %get-tuple-element.10.right), custom_call_target="tpu_custom_call" | custom-call | tf_op jit(solution)/shard_map/update/pallas_call | solution.py:432
Async XLA Ops:
  0.0 37.0 %copy-start = (f32[640,1280]{1,0:T(8,128)S(1)}, f32[640,1280]{1,0:T(8,128)}, u32[]{:S(2)}) copy-start(f32[640,1280]{1,0:T(8,128)} %a.3) | copy-start | bytes 9830404

commit v4 on v3

--- a/solution.py
+++ b/solution.py
@@ -10,7 +10,7 @@
 
 NB = 128
 SUB = 8
-GROUP = 32
+GROUP = 16
 CW = 256
 TILE = 256
 MESH = pl.DeviceIdType.MESH
@@ -48,62 +48,55 @@
     return jnp.broadcast_to(x[:, lane : lane + 1], (SUB, NB))
 
 
-def eliminate(aug, steps):
+def eliminate(work):
     row = lax.broadcasted_iota(jnp.int32, (SUB, NB), 0)
     subs = GROUP // SUB
-    for g in range(NB // GROUP):
-        top = g * GROUP
-        rows = [
-            [[jnp.broadcast_to(block[k : k + 1, h * NB : (h + 1) * NB], (SUB, NB)) for h in range(2)] for k in range(SUB)]
-            for block in (aug[top + s * SUB : top + (s + 1) * SUB, :] for s in range(subs))
-        ]
-        done = []
-        for s in range(subs):
-            lo = top + s * SUB
-            mine = rows[s]
-            wide = 2 * SUB if s + 1 < subs else SUB
-            d = {(k, j): splat(mine[k][0], lo + j) for k in range(SUB) for j in range(k, wide)}
-            for j in range(SUB):
-                inv = lax.rsqrt(d[j, j])
-                for i in range(j + 1, wide):
-                    d[j, i] = d[j, i] * inv
-                for i in range(j + 1, SUB):
-                    for l in range(i, wide):
-                        d[i, l] = d[i, l] - d[j, i] * d[j, l]
-                mine[j] = [x * inv for x in mine[j]]
-                for i in range(j + 1, SUB):
-                    mine[i] = [x - d[j, i] * y for x, y in zip(mine[i], mine[j])]
-            for later in range(s + 1, subs):
-                for i in range(SUB):
-                    for k in range(SUB):
-                        m = d[k, SUB + i] if later == s + 1 else splat(mine[k][0], top + later * SUB + i)
-                        rows[later][i] = [x - m * y for x, y in zip(rows[later][i], mine[k])]
-            halves = []
-            for h in range(2):
-                u = mine[0][h]
-                for k in range(1, SUB):
-                    u = jnp.where(row == k, mine[k][h], u)
-                halves.append(u)
-            done.append(jnp.concatenate(halves, axis=1))
-            if s % 2 and s + 1 < subs:
-                for step in steps.pop(0):
-                    step()
-        u = jnp.concatenate(done, axis=0)
-        aug[top : top + GROUP, :] = u
-        if top + GROUP < NB:
-            h, m, l = split(u)
-            left = jnp.concatenate([h, h, m, h, m, l], axis=0)[:, :NB].astype(bf16)
-            right = jnp.concatenate([h, m, h, l, m, h], axis=0).astype(bf16)
-            taken = lax.dot_general(left, right, (((0,), (0,)), ((), ())), preferred_element_type=f32)
-            aug[top + GROUP :, :] = aug[top + GROUP :, :] - taken[top + GROUP :, :]
-        for step in steps.pop(0):
-            step()
+    rows = [
+        [[jnp.broadcast_to(block[k : k + 1, h * NB : (h + 1) * NB], (SUB, NB)) for h in range(2)] for k in range(SUB)]
+        for block in (work[s * SUB : (s + 1) * SUB, :] for s in range(subs))
+    ]
+    done = []
+    for s in range(subs):
+        mine = rows[s]
+        wide = 2 * SUB if s + 1 < subs else SUB
+        d = {(k, j): splat(mine[k][0], s * SUB + j) for k in range(SUB) for j in range(k, wide)}
+        for j in range(SUB):
+            inv = lax.rsqrt(d[j, j])
+            for i in range(j + 1, wide):
+                d[j, i] = d[j, i] * inv
+            for i in range(j + 1, SUB):
+                for l in range(i, wide):
+                    d[i, l] = d[i, l] - d[j, i] * d[j, l]
+            mine[j] = [x * inv for x in mine[j]]
+            for i in range(j + 1, SUB):
+                mine[i] = [x - d[j, i] * y for x, y in zip(mine[i], mine[j])]
+        for later in range(s + 1, subs):
+            for i in range(SUB):
+                for k in range(SUB):
+                    m = d[k, SUB + i] if later == s + 1 else splat(mine[k][0], later * SUB + i)
+                    rows[later][i] = [x - m * y for x, y in zip(rows[later][i], mine[k])]
+        halves = []
+        for h in range(2):
+            u = mine[0][h]
+            for k in range(1, SUB):
+                u = jnp.where(row == k, mine[k][h], u)
+            halves.append(u)
+        done.append(jnp.concatenate(halves, axis=1))
+    u = jnp.concatenate(done, axis=0)
+    h, m, l = split(u)
+    left = jnp.concatenate([h, h, m, h, m, l], axis=0)[:, :NB].astype(bf16)
+    right = jnp.concatenate([h, m, h, l, m, h], axis=0).astype(bf16)
+    taken = lax.dot_general(left, right, (((0,), (0,)), ((), ())), preferred_element_type=f32)
+    rest = work[GROUP:, :] - taken[GROUP:, :]
+    work[: NB - GROUP, :NB] = pltpu.roll(rest[:, :NB], NB - GROUP, 1)
+    work[: NB - GROUP, NB:] = rest[:, NB:]
+    return u
 
 
 def panels_kernel(
     nrow, ncol, rows_here, cols_here,
     a, panel, left, right,
-    p, ac, k, aug, low,
+    p, ac, k, aug, work, low,
     psend, precv, zsend, ksend, ksib, krecv, asend, arecv, loc,
 ):
     chips = nrow // 2
@@ -145,7 +138,7 @@
     pl.semaphore_signal(barrier, inc=1, device_id=(sib, c), device_id_type=MESH)
     pl.semaphore_wait(barrier, ncol - 1 + chips)
 
-    started = []
+    ending = []
 
     def remote(src, dst, ss, rs, dev):
         return functools.partial(
@@ -157,14 +150,18 @@
         @pl.when(cond)
         def _():
             for make in makes:
-                make().start()
-
-        started.append((cond, makes))
+                if ending:
+                    make().wait_send()
+                else:
+                    make().start()
 
     def incoming(dst, rs):
         return remote(dst, dst, loc.at[3], rs, (sib, c))
 
     def received(cond, *makes):
+        if ending:
+            return
+
         @pl.when(cond)
         def _():
             for make in makes:
@@ -208,9 +205,6 @@
     def own_slab():
         return pltpu.make_async_copy(a.at[pl.ds(0, NB), :], ac.at[core], loc.at[2])
 
-    start((r == 0) & (c == 0), *direct(0))
-    for s in range(2):
-        pl.when(c == s)(own(s).start)
     rest = range(1, nt)
 
     def p_source(here, ts):
@@ -220,15 +214,22 @@
             *[p_copy(1, t, a_rows(t), z, i) for t in ts for i, z in enumerate((0, 2) if ncol > 2 else (0,))],
         )
 
-    received((r == 0) & (c != 0), p_in(0, 0))
-    for s in range(2):
-        pl.when(c == s)(own(s).wait)
-    start(r == 0, *spread(0, pc(0, 0)))
-    pl.when(source)(lambda: own_slab().start())
-    p_source(q != 0, range(nt))
-    received((q != 0) & first, incoming(k.at[0], krecv.at[0]))
-    start((q != 0) & first, remote(k.at[0], k.at[0], ksib.at[0], krecv.at[0], (sib, c)))
-    received(second, incoming(k.at[0], krecv.at[0]))
+    def opening():
+        start((r == 0) & (c == 0), *direct(0))
+        if not ending:
+            for s in range(2):
+                pl.when(c == s)(own(s).start)
+        received((r == 0) & (c != 0), p_in(0, 0))
+        if not ending:
+            for s in range(2):
+                pl.when(c == s)(own(s).wait)
+        start(r == 0, *spread(0, pc(0, 0)))
+        p_source(q != 0, range(nt))
+        received((q != 0) & first, incoming(k.at[0], krecv.at[0]))
+        start((q != 0) & first, remote(k.at[0], k.at[0], ksib.at[0], krecv.at[0], (sib, c)))
+        received(second, incoming(k.at[0], krecv.at[0]))
+        if not ending:
+            pl.when(source)(lambda: own_slab().start())
 
     def p_pass(t, z):
         here = (c == 1) if z == 1 else (c > 1) & (c < ncol - 1)
@@ -266,7 +267,7 @@
             start(here & (pos < chips - 1), over)
             start(here, across)
 
-    half = NB // (2 * SUB)
+    half = NB // GROUP
     places = [[] for _ in range(2 * half)]
 
     def put(at, *step):
@@ -286,6 +287,8 @@
         for at in range(1, min(chips, 4)):
             put(2 + 1.5 * t + 2 * (at - 1), a_pass, t, at)
 
+    opening()
+
     eye = jnp.where(
         lax.broadcasted_iota(jnp.int32, (NB, NB), 0) == lax.broadcasted_iota(jnp.int32, (NB, NB), 1),
         f32(1.0), f32(0.0),
@@ -293,28 +296,46 @@
 
     @pl.when(r == 0)
     def _():
-        aug[0, :, :NB] = p[0, :NB, :]
+        work[:, :NB] = p[0, :NB, :]
 
     @pl.when(r != 0)
     def _():
-        aug[0, :, :NB] = k[0]
-
-    aug[0, :, NB:] = eye
-    eliminate(aug.at[0], places[:half])
-
-    received(first, *[incoming(k.at[s], krecv.at[s]) for s in (1, 2)])
-
-    @pl.when(r == 1)
-    def _():
-        k[1] = p[0, :NB, :]
-        k[2] = p[1, :NB, :]
-
+        work[:, :NB] = k[0]
+
+    work[:, NB:] = eye
+
+    def second_block():
+        received(first, *[incoming(k.at[s], krecv.at[s]) for s in (1, 2)])
+
+        @pl.when(r == 1)
+        def _():
+            k[1] = p[0, :NB, :]
+            k[2] = p[1, :NB, :]
+
+        l10 = dot(k[1], aug[0, :, NB:], 1, 1)
+        low[...] = l10
+        work[:, :NB] = k[2] - dot(l10, l10, 1, 1)
+        work[:, NB:] = eye
+
+    def group(g, carry):
+        pl.when(g == half)(second_block)
+        u = eliminate(work)
+        h = g // half
+        top = lax.rem(g, half) * GROUP
+        here = pl.ds(pl.multiple_of(top, GROUP), GROUP)
+        aug[h, here, :NB] = pltpu.roll(u[:, :NB], top, 1)
+        aug[h, here, NB:] = u[:, NB:]
+        for at, steps in enumerate(places):
+            if steps:
+                @pl.when(g == at)
+                def _():
+                    for step in steps:
+                        step()
+        return carry
+
+    lax.fori_loop(0, 2 * half, group, 0)
     w0 = aug[0, :, NB:]
-    low[...] = dot(k[1], w0, 1, 1)
     l10 = low[...]
-    aug[1, :, :NB] = k[2] - dot(l10, l10, 1, 1)
-    aug[1, :, NB:] = eye
-    eliminate(aug.at[1], places[half:])
 
     w1 = aug[1, :, NB:]
     w10 = -dot(w1, dot(l10, w0))
@@ -334,12 +355,17 @@
     received((r == 0) & (c != 1), p_in(1, 0))
     pl.when(source)(lambda: own_slab().wait())
 
-    rh0, rl0 = two(p[0])
-    rh1, rl1 = two(p[1])
-    rows = mm(jnp.concatenate([rh0, rh1, rl0, rl1, rh0, rh1], axis=1), w_right)
-    panel[...] = rows
-    rh, rl = two(rows)
-    left[...] = jnp.concatenate([rh, rl, rh], axis=1)
+    def rows_part(t, carry):
+        here = pl.ds(pl.multiple_of(t * NB, NB), NB)
+        rh0, rl0 = two(p[0, here, :])
+        rh1, rl1 = two(p[1, here, :])
+        rows = mm(jnp.concatenate([rh0, rh1, rl0, rl1, rh0, rh1], axis=1), w_right)
+        panel[here, :] = rows
+        rh, rl = two(rows)
+        left[here, :] = jnp.concatenate([rh, rl, rh], axis=1)
+        return carry
+
+    lax.fori_loop(0, nt, rows_part, 0)
 
     upper = lax.broadcasted_iota(jnp.int32, (NB, NB), 0) <= lax.broadcasted_iota(jnp.int32, (NB, NB), 1)
 
@@ -352,45 +378,53 @@
     def _():
         panel[:NB, NB:] = jnp.where(upper, aug[1, :, :NB], f32(0.0)).T
 
-    for t in range(na):
-        incoming(ach(1 - core, t), arecv.at[1 - core, t])().wait_recv()
-        here = slice(t * CW, (t + 1) * CW)
+    def cols_part(t, carry):
+        here = pl.ds(pl.multiple_of(t * CW, CW), CW)
+        incoming(ac.at[1 - core, :, here], arecv.at[1 - core, t])().wait_recv()
         h0, l0 = two(ac[0, :, here])
         h1, l1 = two(ac[1, :, here])
         cols = mm(w_left, jnp.concatenate([h0, h1, h0, h1, l0, l1], axis=0))
         ch, cl = two(cols)
         right[:, here] = jnp.concatenate([ch, ch, cl], axis=0)
-
-    for cond, makes in started:
-        @pl.when(cond)
-        def _():
-            for make in makes:
-                make().wait_send()
+        return carry
+
+    lax.fori_loop(0, na, cols_part, 0)
+
+    ending.append(True)
+    opening()
+    for steps in places:
+        for step in steps:
+            step()
 
 
 def update_kernel(a, panel, left, right, out, held, sems):
     r = lax.axis_index("row")
     c = lax.axis_index("col")
-    copies = []
-    for t in range(a.shape[1] // TILE):
-        here = pl.ds(t * TILE, TILE)
+
+    def copy(t):
+        here = pl.ds(pl.multiple_of(t * TILE, TILE), TILE)
+        return pltpu.make_async_copy(held.at[:, here], out.at[:, here], sems.at[t])
+
+    def tile(t, carry):
+        here = pl.ds(pl.multiple_of(t * TILE, TILE), TILE)
         held[:, here] = a[:, here] - mm(left[...], right[:, here])
 
         @pl.when(r < 2)
         def _():
             held[:NB, here] = jnp.zeros((NB, TILE), f32)
 
-        if t == 0:
-            for s in range(2):
-                @pl.when(c == s)
-                def _():
-                    held[:, :NB] = panel[:, s * NB : (s + 1) * NB]
-
-        copy = pltpu.make_async_copy(held.at[:, here], out.at[:, here], sems.at[t])
-        copy.start()
-        copies.append(copy)
-    for copy in copies:
-        copy.wait()
+        for s in range(2):
+            @pl.when((t == 0) & (c == s))
+            def _():
+                held[:, :NB] = panel[:, s * NB : (s + 1) * NB]
+
+        copy(t).start()
+        return carry
+
+    tiles = a.shape[1] // TILE
+    lax.fori_loop(0, tiles, tile, 0)
+    for t in range(tiles):
+        copy(t).wait()
 
 
 def local(nrow, ncol, kernel):
@@ -413,6 +447,7 @@
             pltpu.VMEM((2, NB, cols), f32),
             pltpu.VMEM((3, NB, NB), f32),
             pltpu.VMEM((2, NB, 2 * NB), f32),
+            pltpu.VMEM((NB, 2 * NB), f32),
             pltpu.VMEM((NB, NB), f32),
             dma((2, nt, 2)),
             dma((2, nt)),

time: 41.3 us -> 41.4 us (level)
    pallas_call x1, Pallas kernels: 37 us -> 38.1 us  [local(): pl.pallas_call(functools.partial(panels_kernel, nrow, ncol, rows, cols),...]
    pallas_call x1, Pallas kernels: 3.94 us -> 3.11 us  [local(): pl.pallas_call(update_kernel, out_shape=jax.ShapeDtypeStruct((rows, cols)...]
where the time goes in v4:
time: 41.4 us; the launch traced here: 41.3 us
  Pallas kernels  41.3 us (100%)
    pallas_call x1, Pallas kernels, local(): pl.pallas_call(functools.partial(panels_kernel, nrow, ncol, rows, cols),...  38.1 us
    pallas_call x1, Pallas kernels, local(): pl.pallas_call(update_kernel, out_shape=jax.ShapeDtypeStruct((rows, cols)...  3.11 us

profile of v4, /device:TPU:20, one launch (start us, length us, event | category | flops | bytes accessed | tf_op | source)
XLA Modules:
  0.0 41.3 jit_solution(9391399372937940285)
XLA Ops:
  0.0 0.0 copy-start
  0.0 38.1 %panels.1 = (f32[640,256]{1,0:T(8,128)S(1)}, bf16[640,768]{1,0:T(8,128)(2,1)S(1)}, bf16[768,1280]{1,0:T(8,128)(2,1)S(1)}) custom-call(f32[640,1280]{1,0:T(8,128)} %a.3), custom_call_target="tpu_custom_call" | custom-call | tf_op jit(solution)/shard_map/panels/pallas_call | solution.py:436
  38.2 0.0 copy-done
  38.2 3.1 %update.1 = f32[640,1280]{1,0:T(8,128)} custom-call(f32[640,1280]{1,0:T(8,128)S(1)} %copy-done, f32[640,256]{1,0:T(8,128)S(1)} %get-tuple-element.8.panel, bf16[640,768]{1,0:T(8,128)(2,1)S(1)} %get-tuple-element.9.left, bf16[768,1280]{1,0:T(8,128)(2,1)S(1)} %get-tuple-element.10.right), custom_call_target="tpu_custom_call" | custom-call | tf_op jit(solution)/shard_map/update/pallas_call | solution.py:467
Async XLA Ops:
  0.0 38.2 %copy-start = (f32[640,1280]{1,0:T(8,128)S(1)}, f32[640,1280]{1,0:T(8,128)}, u32[]{:S(2)}) copy-start(f32[640,1280]{1,0:T(8,128)} %a.3) | copy-start | bytes 9830404

commit v5 on v4

--- a/solution.py
+++ b/solution.py
@@ -10,7 +10,7 @@
 
 NB = 128
 SUB = 8
-GROUP = 16
+GROUP = 32
 CW = 256
 TILE = 256
 MESH = pl.DeviceIdType.MESH
@@ -48,7 +48,7 @@
     return jnp.broadcast_to(x[:, lane : lane + 1], (SUB, NB))
 
 
-def eliminate(work):
+def eliminate(work, midway):
     row = lax.broadcasted_iota(jnp.int32, (SUB, NB), 0)
     subs = GROUP // SUB
     rows = [
@@ -82,6 +82,8 @@
                 u = jnp.where(row == k, mine[k][h], u)
             halves.append(u)
         done.append(jnp.concatenate(halves, axis=1))
+        if s == subs // 2 - 1:
+            midway()
     u = jnp.concatenate(done, axis=0)
     h, m, l = split(u)
     left = jnp.concatenate([h, h, m, h, m, l], axis=0)[:, :NB].astype(bf16)
@@ -97,7 +99,7 @@
     nrow, ncol, rows_here, cols_here,
     a, panel, left, right,
     p, ac, k, aug, work, low,
-    psend, precv, zsend, ksend, ksib, krecv, asend, arecv, loc,
+    psend, precv, zsend, ksend, ksib, krecv, asend, arecv, slab, loc,
 ):
     chips = nrow // 2
     nx = math.isqrt(chips)
@@ -171,7 +173,7 @@
         return p.at[s, pl.ds(t * NB, NB)]
 
     def ach(s, t):
-        return ac.at[s, :, pl.ds(t * CW, CW)]
+        return ac.at[s, t]
 
     def a_rows(t):
         return a.at[pl.ds(t * NB, NB), pl.ds(0, NB)]
@@ -190,9 +192,9 @@
 
     def spread(s, src):
         base = 0 if s == 0 else 1
-        return [
+        return [remote(src, k.at[s], ksib.at[s], krecv.at[s], (sib, c))] + [
             remote(src, k.at[s], ksend.at[s, j], krecv.at[s], (2 * j + base, c)) for j in range(chips - 1, 0, -1)
-        ] + [remote(src, k.at[s], ksib.at[s], krecv.at[s], (sib, c))]
+        ]
 
     def a_copies(t, src):
         over = remote(src, ach(core, t), asend.at[t, 0], arecv.at[core, t], (onward, c))
@@ -203,15 +205,17 @@
         return pltpu.make_async_copy(a.at[:, pl.ds(0, NB)], p.at[s], loc.at[s])
 
     def own_slab():
-        return pltpu.make_async_copy(a.at[pl.ds(0, NB), :], ac.at[core], loc.at[2])
+        return [
+            pltpu.make_async_copy(a.at[pl.ds(0, NB), pl.ds(t * CW, CW)], ach(core, t), slab.at[t]) for t in range(na)
+        ]
 
     rest = range(1, nt)
 
     def p_source(here, ts):
-        start(here & (c == 0), *[p_copy(0, t, a_rows(t), 1) for t in ts])
+        start(here & (c == 0), *[p_copy(0, t, pc(0, t), 1) for t in ts])
         start(
             here & (c == 1),
-            *[p_copy(1, t, a_rows(t), z, i) for t in ts for i, z in enumerate((0, 2) if ncol > 2 else (0,))],
+            *[p_copy(1, t, pc(1, t), z, i) for t in ts for i, z in enumerate((0, 2) if ncol > 2 else (0,))],
         )
 
     def opening():
@@ -229,7 +233,7 @@
         start((q != 0) & first, remote(k.at[0], k.at[0], ksib.at[0], krecv.at[0], (sib, c)))
         received(second, incoming(k.at[0], krecv.at[0]))
         if not ending:
-            pl.when(source)(lambda: own_slab().start())
+            pl.when(source)(lambda: [copy.start() for copy in own_slab()] and None)
 
     def p_pass(t, z):
         here = (c == 1) if z == 1 else (c > 1) & (c < ncol - 1)
@@ -241,7 +245,7 @@
 
     def direct_rest():
         start((r == 1) & (c == 0), *direct(0))
-        start(source & (c == 1), *direct(1))
+        start((r == 1) & (c == 1), *direct(1))
 
     def corner_rest():
         received((r == 1) & (c != 0), p_in(0, 0))
@@ -254,7 +258,9 @@
         start(here, *[remote(k.at[s], k.at[s], ksib.at[s], krecv.at[s], (sib, c)) for s in (1, 2)])
 
     def a_source():
-        makes = [a_copies(t, a.at[pl.ds(0, NB), pl.ds(t * CW, CW)]) for t in range(na)]
+        if not ending:
+            pl.when(source)(lambda: [copy.wait() for copy in own_slab()] and None)
+        makes = [a_copies(t, ach(core, t)) for t in range(na)]
         start(source, *[make for pair in makes for make in pair])
 
     def a_pass(t, at):
@@ -268,14 +274,14 @@
             start(here, across)
 
     half = NB // GROUP
-    places = [[] for _ in range(2 * half)]
+    places = [[] for _ in range(4 * half)]
 
     def put(at, *step):
-        places[min(int(at), 2 * half - 1)].append(functools.partial(*step))
+        places[min(int(at), 4 * half - 1)].append(functools.partial(*step))
 
     put(0, direct_rest)
     put(1, p_source, source, rest)
-    put(1, a_source)
+    put(0, a_source)
     put(2, corner_rest)
     put(5, corner_pass)
     for t in range(nt):
@@ -319,18 +325,22 @@
 
     def group(g, carry):
         pl.when(g == half)(second_block)
-        u = eliminate(work)
+
+        def visit(odd):
+            for at, steps in enumerate(places):
+                if steps and at % 2 == odd:
+                    @pl.when(g == at // 2)
+                    def _():
+                        for step in steps:
+                            step()
+
+        u = eliminate(work, functools.partial(visit, 0))
         h = g // half
         top = lax.rem(g, half) * GROUP
         here = pl.ds(pl.multiple_of(top, GROUP), GROUP)
         aug[h, here, :NB] = pltpu.roll(u[:, :NB], top, 1)
         aug[h, here, NB:] = u[:, NB:]
-        for at, steps in enumerate(places):
-            if steps:
-                @pl.when(g == at)
-                def _():
-                    for step in steps:
-                        step()
+        visit(1)
         return carry
 
     lax.fori_loop(0, 2 * half, group, 0)
@@ -352,8 +362,6 @@
     received((c == 0) | (last & (c > 1)), *[p_in(1, t) for t in rest])
     received((q != 0) & last, p_in(0, 0))
     received((q != 0) & ((c == 0) | (last & (c > 1))), p_in(1, 0))
-    received((r == 0) & (c != 1), p_in(1, 0))
-    pl.when(source)(lambda: own_slab().wait())
 
     def rows_part(t, carry):
         here = pl.ds(pl.multiple_of(t * NB, NB), NB)
@@ -380,9 +388,9 @@
 
     def cols_part(t, carry):
         here = pl.ds(pl.multiple_of(t * CW, CW), CW)
-        incoming(ac.at[1 - core, :, here], arecv.at[1 - core, t])().wait_recv()
-        h0, l0 = two(ac[0, :, here])
-        h1, l1 = two(ac[1, :, here])
+        incoming(ac.at[1 - core, t], arecv.at[1 - core, t])().wait_recv()
+        h0, l0 = two(ac[0, t])
+        h1, l1 = two(ac[1, t])
         cols = mm(w_left, jnp.concatenate([h0, h1, h0, h1, l0, l1], axis=0))
         ch, cl = two(cols)
         right[:, here] = jnp.concatenate([ch, ch, cl], axis=0)
@@ -444,7 +452,7 @@
         out_specs=[pl.BlockSpec(memory_space=pltpu.VMEM)] * 3,
         scratch_shapes=[
             pltpu.VMEM((2, rows, NB), f32),
-            pltpu.VMEM((2, NB, cols), f32),
+            pltpu.VMEM((2, na, NB, CW), f32),
             pltpu.VMEM((3, NB, NB), f32),
             pltpu.VMEM((2, NB, 2 * NB), f32),
             pltpu.VMEM((NB, 2 * NB), f32),
@@ -457,6 +465,7 @@
             dma((3,)),
             dma((na, 2)),
             dma((2, na)),
+            dma((na,)),
             dma((4,)),
         ],
         compiler_params=pltpu.CompilerParams(

time: 41.4 us -> 40.9 us (0.988)
  Pallas kernels: 41.3 us -> 40.8 us
    pallas_call x1, Pallas kernels: 38.1 us -> 37.6 us  [local(): pl.pallas_call(functools.partial(panels_kernel, nrow, ncol, rows, cols),...]
where the time goes in v5:
time: 40.9 us; the launch traced here: 40.8 us
  Pallas kernels  40.8 us (100%)
    pallas_call x1, Pallas kernels, local(): pl.pallas_call(functools.partial(panels_kernel, nrow, ncol, rows, cols),...  37.6 us
    pallas_call x1, Pallas kernels, local(): pl.pallas_call(update_kernel, out_shape=jax.ShapeDtypeStruct((rows, cols)...  3.1 us

profile of v5, /device:TPU:20, one launch (start us, length us, event | category | flops | bytes accessed | tf_op | source)
XLA Modules:
  0.0 40.8 jit_solution(12135353823149367184)
XLA Ops:
  0.0 0.0 copy-start
  0.0 37.6 %panels.1 = (f32[640,256]{1,0:T(8,128)S(1)}, bf16[640,768]{1,0:T(8,128)(2,1)S(1)}, bf16[768,1280]{1,0:T(8,128)(2,1)S(1)}) custom-call(f32[640,1280]{1,0:T(8,128)} %a.3), custom_call_target="tpu_custom_call" | custom-call | tf_op jit(solution)/shard_map/panels/pallas_call | solution.py:444
  37.7 0.0 copy-done
  37.7 3.1 %update.1 = f32[640,1280]{1,0:T(8,128)} custom-call(f32[640,1280]{1,0:T(8,128)S(1)} %copy-done, f32[640,256]{1,0:T(8,128)S(1)} %get-tuple-element.8.panel, bf16[640,768]{1,0:T(8,128)(2,1)S(1)} %get-tuple-element.9.left, bf16[768,1280]{1,0:T(8,128)(2,1)S(1)} %get-tuple-element.10.right), custom_call_target="tpu_custom_call" | custom-call | tf_op jit(solution)/shard_map/update/pallas_call | solution.py:476
Async XLA Ops:
  0.0 37.7 %copy-start = (f32[640,1280]{1,0:T(8,128)S(1)}, f32[640,1280]{1,0:T(8,128)}, u32[]{:S(2)}) copy-start(f32[640,1280]{1,0:T(8,128)} %a.3) | copy-start | bytes 9830404

commit v6 on v5

--- a/solution.py
+++ b/solution.py
@@ -227,6 +227,8 @@
         if not ending:
             for s in range(2):
                 pl.when(c == s)(own(s).wait)
+        start((r == 1) & (c == 1), *direct(1))
+        p_source(source & (c == 1), rest)
         start(r == 0, *spread(0, pc(0, 0)))
         p_source(q != 0, range(nt))
         received((q != 0) & first, incoming(k.at[0], krecv.at[0]))
@@ -235,17 +237,15 @@
         if not ending:
             pl.when(source)(lambda: [copy.start() for copy in own_slab()] and None)
 
-    def p_pass(t, z):
+    def p_pass(t, s, z):
         here = (c == 1) if z == 1 else (c > 1) & (c < ncol - 1)
         if t == 0:
             here = here & (q != 0)
-        panels = (0,) if z == 1 else (0, 1)
-        received(here, *[p_in(s, t) for s in panels])
-        start(here, *[p_copy(s, t, pc(s, t), c + 1) for s in panels])
+        received(here, p_in(s, t))
+        start(here, p_copy(s, t, pc(s, t), c + 1))
 
     def direct_rest():
         start((r == 1) & (c == 0), *direct(0))
-        start((r == 1) & (c == 1), *direct(1))
 
     def corner_rest():
         received((r == 1) & (c != 0), p_in(0, 0))
@@ -280,18 +280,19 @@
         places[min(int(at), 4 * half - 1)].append(functools.partial(*step))
 
     put(0, direct_rest)
-    put(1, p_source, source, rest)
+    put(0, p_source, source & (c == 0), rest)
     put(0, a_source)
     put(2, corner_rest)
     put(5, corner_pass)
     for t in range(nt):
         if ncol > 2:
-            put(1 + 2 * t, p_pass, t, 1)
+            put(1 + 2 * t, p_pass, t, 0, 1)
         if ncol > 3:
-            put(2 + 2 * t, p_pass, t, 2)
+            put(2 + 2 * t, p_pass, t, 1, 2)
+            put(5 + 3 * t, p_pass, t, 0, 2)
     for t in range(na):
         for at in range(1, min(chips, 4)):
-            put(2 + 1.5 * t + 2 * (at - 1), a_pass, t, at)
+            put(2 + 1.8 * t + 2.6 * (at - 1), a_pass, t, at)
 
     opening()
 
@@ -357,35 +358,6 @@
     wh, wl = two(w.T)
     w_right = jnp.concatenate([wh, wh, wl], axis=0)
 
-    last = c == ncol - 1
-    received(last & (c > 0), *[p_in(0, t) for t in rest])
-    received((c == 0) | (last & (c > 1)), *[p_in(1, t) for t in rest])
-    received((q != 0) & last, p_in(0, 0))
-    received((q != 0) & ((c == 0) | (last & (c > 1))), p_in(1, 0))
-
-    def rows_part(t, carry):
-        here = pl.ds(pl.multiple_of(t * NB, NB), NB)
-        rh0, rl0 = two(p[0, here, :])
-        rh1, rl1 = two(p[1, here, :])
-        rows = mm(jnp.concatenate([rh0, rh1, rl0, rl1, rh0, rh1], axis=1), w_right)
-        panel[here, :] = rows
-        rh, rl = two(rows)
-        left[here, :] = jnp.concatenate([rh, rl, rh], axis=1)
-        return carry
-
-    lax.fori_loop(0, nt, rows_part, 0)
-
-    upper = lax.broadcasted_iota(jnp.int32, (NB, NB), 0) <= lax.broadcasted_iota(jnp.int32, (NB, NB), 1)
-
-    @pl.when(r == 0)
-    def _():
-        panel[:NB, :NB] = jnp.where(upper, aug[0, :, :NB], f32(0.0)).T
-        panel[:NB, NB:] = jnp.zeros((NB, NB), f32)
-
-    @pl.when(r == 1)
-    def _():
-        panel[:NB, NB:] = jnp.where(upper, aug[1, :, :NB], f32(0.0)).T
-
     def cols_part(t, carry):
         here = pl.ds(pl.multiple_of(t * CW, CW), CW)
         incoming(ac.at[1 - core, t], arecv.at[1 - core, t])().wait_recv()
@@ -397,6 +369,37 @@
         return carry
 
     lax.fori_loop(0, na, cols_part, 0)
+
+    @pl.when(r == 0)
+    def _():
+        p[1, :NB, :] = jnp.zeros((NB, NB), f32)
+
+    def rows_part(t, carry):
+        here = pl.ds(pl.multiple_of(t * NB, NB), NB)
+        sent = (t > 0) | (q != 0)
+        last = c == ncol - 1
+        received(last & sent, p_in(0, t))
+        received(((c == 0) | (last & (c > 1))) & sent, p_in(1, t))
+        rh0, rl0 = two(p[0, here, :])
+        rh1, rl1 = two(p[1, here, :])
+        rows = mm(jnp.concatenate([rh0, rh1, rl0, rl1, rh0, rh1], axis=1), w_right)
+        panel[here, :] = rows
+        rh, rl = two(rows)
+        left[here, :] = jnp.concatenate([rh, rl, rh], axis=1)
+        return carry
+
+    lax.fori_loop(0, nt, rows_part, 0)
+
+    upper = lax.broadcasted_iota(jnp.int32, (NB, NB), 0) <= lax.broadcasted_iota(jnp.int32, (NB, NB), 1)
+
+    @pl.when(r == 0)
+    def _():
+        panel[:NB, :NB] = jnp.where(upper, aug[0, :, :NB], f32(0.0)).T
+        panel[:NB, NB:] = jnp.zeros((NB, NB), f32)
+
+    @pl.when(r == 1)
+    def _():
+        panel[:NB, NB:] = jnp.where(upper, aug[1, :, :NB], f32(0.0)).T
 
     ending.append(True)
     opening()

time: 40.9 us -> 39.1 us (0.956)
  the two profiles are of different devices: /device:TPU:20 before, /device:TPU:12 now
where the time goes in v6:
time: 39.1 us; the launch traced here: 39 us
  Pallas kernels  39 us (100%)
    pallas_call x1, Pallas kernels, local(): pl.pallas_call(functools.partial(panels_kernel, nrow, ncol, rows, cols),...  35.8 us
    pallas_call x1, Pallas kernels, local(): pl.pallas_call(update_kernel, out_shape=jax.ShapeDtypeStruct((rows, cols)...  3.12 us

profile of v6, /device:TPU:12, one launch (start us, length us, event | category | flops | bytes accessed | tf_op | source)
XLA Modules:
  0.0 39.0 jit_solution(5475981109291413287)
XLA Ops:
  0.0 0.0 copy-start
  0.0 35.8 %panels.1 = (f32[640,256]{1,0:T(8,128)S(1)}, bf16[640,768]{1,0:T(8,128)(2,1)S(1)}, bf16[768,1280]{1,0:T(8,128)(2,1)S(1)}) custom-call(f32[640,1280]{1,0:T(8,128)} %a.3), custom_call_target="tpu_custom_call" | custom-call | tf_op jit(solution)/shard_map/panels/pallas_call | solution.py:447
  35.8 0.0 copy-done
  35.9 3.1 %update.1 = f32[640,1280]{1,0:T(8,128)} custom-call(f32[640,1280]{1,0:T(8,128)S(1)} %copy-done, f32[640,256]{1,0:T(8,128)S(1)} %get-tuple-element.8.panel, bf16[640,768]{1,0:T(8,128)(2,1)S(1)} %get-tuple-element.9.left, bf16[768,1280]{1,0:T(8,128)(2,1)S(1)} %get-tuple-element.10.right), custom_call_target="tpu_custom_call" | custom-call | tf_op jit(solution)/shard_map/update/pallas_call | solution.py:479
Async XLA Ops:
  0.0 35.8 %copy-start = (f32[640,1280]{1,0:T(8,128)S(1)}, f32[640,1280]{1,0:T(8,128)}, u32[]{:S(2)}) copy-start(f32[640,1280]{1,0:T(8,128)} %a.3) | copy-start | bytes 9830404

commit v7 on v6

--- a/solution.py
+++ b/solution.py
@@ -117,18 +117,13 @@
     second = core == 1
     source = q == 0
 
-    oy = lax.rem(qy, 2)
-    ox = lax.rem(qx, 2)
-    if nx > 1 and ny > 1:
-        pos_x = qy * nx + qx + oy * (nx - 1 - 2 * qx)
-        pos_y = qx * ny + qy + ox * (ny - 1 - 2 * qy)
-        step_x = jnp.where(oy == 0, jnp.where(qx < nx - 1, 1, nx), jnp.where(qx > 0, -1, nx))
-        step_y = jnp.where(ox == 0, jnp.where(qy < ny - 1, nx, 1), jnp.where(qy > 0, -nx, 1))
-        pos = jnp.where(first, pos_x, pos_y)
-        onward = lax.rem(r + 2 * jnp.where(first, step_x, step_y) + nrow, nrow)
-    else:
-        pos = q
-        onward = lax.rem(r + 2, nrow)
+    depth = qx + qy
+    far_x = qx < nx - 1
+    far_y = qy < ny - 1
+    to_x = far_x & (first | (qy == 0))
+    to_y = far_y & (second | (qx == 0))
+    next_x = lax.rem(r + 2, nrow)
+    next_y = lax.rem(r + 2 * nx, nrow)
 
     barrier = pltpu.get_barrier_semaphore()
     for i in range(1, ncol):
@@ -196,10 +191,15 @@
             remote(src, k.at[s], ksend.at[s, j], krecv.at[s], (2 * j + base, c)) for j in range(chips - 1, 0, -1)
         ]
 
-    def a_copies(t, src):
-        over = remote(src, ach(core, t), asend.at[t, 0], arecv.at[core, t], (onward, c))
-        across = remote(src, ach(core, t), asend.at[t, 1], arecv.at[core, t], (sib, c))
-        return over, across
+    def a_send(here, t):
+        src = ach(core, t)
+
+        def to(way, row):
+            return remote(src, src, asend.at[t, way], arecv.at[core, t], (row, c))
+
+        start(here & to_x, to(0, next_x))
+        start(here & to_y, to(1, next_y))
+        start(here, to(2, sib))
 
     def own(s):
         return pltpu.make_async_copy(a.at[:, pl.ds(0, NB)], p.at[s], loc.at[s])
@@ -228,11 +228,12 @@
             for s in range(2):
                 pl.when(c == s)(own(s).wait)
         start((r == 1) & (c == 1), *direct(1))
-        p_source(source & (c == 1), rest)
         start(r == 0, *spread(0, pc(0, 0)))
-        p_source(q != 0, range(nt))
+        p_source((q != 0) & second, range(nt))
         received((q != 0) & first, incoming(k.at[0], krecv.at[0]))
         start((q != 0) & first, remote(k.at[0], k.at[0], ksib.at[0], krecv.at[0], (sib, c)))
+        p_source((q != 0) & first, range(nt))
+        p_source(source & (c == 1), rest)
         received(second, incoming(k.at[0], krecv.at[0]))
         if not ending:
             pl.when(source)(lambda: [copy.start() for copy in own_slab()] and None)
@@ -260,18 +261,13 @@
     def a_source():
         if not ending:
             pl.when(source)(lambda: [copy.wait() for copy in own_slab()] and None)
-        makes = [a_copies(t, ach(core, t)) for t in range(na)]
-        start(source, *[make for pair in makes for make in pair])
+        for t in range(na):
+            a_send(source, t)
 
     def a_pass(t, at):
-        here = pos == at if at < 3 else pos >= at
-        over, across = a_copies(t, ach(core, t))
+        here = depth == at if at < 3 else depth >= at
         received(here, incoming(ach(core, t), arecv.at[core, t]))
-        if at < 3:
-            start(here, over, across)
-        else:
-            start(here & (pos < chips - 1), over)
-            start(here, across)
+        a_send(here, t)
 
     half = NB // GROUP
     places = [[] for _ in range(4 * half)]
@@ -291,8 +287,8 @@
             put(2 + 2 * t, p_pass, t, 1, 2)
             put(5 + 3 * t, p_pass, t, 0, 2)
     for t in range(na):
-        for at in range(1, min(chips, 4)):
-            put(2 + 1.8 * t + 2.6 * (at - 1), a_pass, t, at)
+        for at in range(1, min(nx + ny - 1, 4)):
+            put(2 * t + 2 * at, a_pass, t, at)
 
     opening()
 
@@ -466,7 +462,7 @@
             dma((3, chips)),
             dma((3,)),
             dma((3,)),
-            dma((na, 2)),
+            dma((na, 3)),
             dma((2, na)),
             dma((na,)),
             dma((4,)),

time: 39.1 us -> 45.4 us (1.16)
  the two profiles are of different devices: /device:TPU:12 before, /device:TPU:15 now
where the time goes in v7:
time: 45.4 us; the launch traced here: 45.3 us
  Pallas kernels  45.2 us (100%)
    pallas_call x1, Pallas kernels, local(): pl.pallas_call(functools.partial(panels_kernel, nrow, ncol, rows, cols),...  42.1 us
    pallas_call x1, Pallas kernels, local(): pl.pallas_call(update_kernel, out_shape=jax.ShapeDtypeStruct((rows, cols)...  3.12 us

profile of v7, /device:TPU:15, one launch (start us, length us, event | category | flops | bytes accessed | tf_op | source)
XLA Modules:
  0.0 45.3 jit_solution(3646306582037907032)
XLA Ops:
  0.0 0.0 copy-start
  0.0 42.1 %panels.1 = (f32[640,256]{1,0:T(8,128)S(1)}, bf16[640,768]{1,0:T(8,128)(2,1)S(1)}, bf16[768,1280]{1,0:T(8,128)(2,1)S(1)}) custom-call(f32[640,1280]{1,0:T(8,128)} %a.3), custom_call_target="tpu_custom_call" | custom-call | tf_op jit(solution)/shard_map/panels/pallas_call | solution.py:443
  42.1 0.0 copy-done
  42.1 3.1 %update.1 = f32[640,1280]{1,0:T(8,128)} custom-call(f32[640,1280]{1,0:T(8,128)S(1)} %copy-done, f32[640,256]{1,0:T(8,128)S(1)} %get-tuple-element.8.panel, bf16[640,768]{1,0:T(8,128)(2,1)S(1)} %get-tuple-element.9.left, bf16[768,1280]{1,0:T(8,128)(2,1)S(1)} %get-tuple-element.10.right), custom_call_target="tpu_custom_call" | custom-call | tf_op jit(solution)/shard_map/update/pallas_call | solution.py:475
Async XLA Ops:
  0.0 42.1 %copy-start = (f32[640,1280]{1,0:T(8,128)S(1)}, f32[640,1280]{1,0:T(8,128)}, u32[]{:S(2)}) copy-start(f32[640,1280]{1,0:T(8,128)} %a.3) | copy-start | bytes 9830404

commit v8 on v6

--- a/solution.py
+++ b/solution.py
@@ -11,7 +11,7 @@
 NB = 128
 SUB = 8
 GROUP = 32
-CW = 256
+CW = 128
 TILE = 256
 MESH = pl.DeviceIdType.MESH
 f32 = jnp.float32
@@ -228,11 +228,12 @@
             for s in range(2):
                 pl.when(c == s)(own(s).wait)
         start((r == 1) & (c == 1), *direct(1))
-        p_source(source & (c == 1), rest)
         start(r == 0, *spread(0, pc(0, 0)))
-        p_source(q != 0, range(nt))
+        p_source((q != 0) & second, range(nt))
         received((q != 0) & first, incoming(k.at[0], krecv.at[0]))
         start((q != 0) & first, remote(k.at[0], k.at[0], ksib.at[0], krecv.at[0], (sib, c)))
+        p_source((q != 0) & first, range(nt))
+        p_source(source & (c == 1), rest)
         received(second, incoming(k.at[0], krecv.at[0]))
         if not ending:
             pl.when(source)(lambda: [copy.start() for copy in own_slab()] and None)
@@ -292,7 +293,7 @@
             put(5 + 3 * t, p_pass, t, 0, 2)
     for t in range(na):
         for at in range(1, min(chips, 4)):
-            put(2 + 1.8 * t + 2.6 * (at - 1), a_pass, t, at)
+            put(1.5 + 0.9 * t + 1.8 * (at - 1), a_pass, t, at)
 
     opening()
 

time: 39.1 us -> 41.3 us (1.056)
  the two profiles are of different devices: /device:TPU:12 before, /device:TPU:20 now
where the time goes in v8:
time: 41.3 us; the launch traced here: 41 us
  Pallas kernels  41 us (99%)
    pallas_call x1, Pallas kernels, local(): pl.pallas_call(functools.partial(panels_kernel, nrow, ncol, rows, cols),...  37.9 us
    pallas_call x1, Pallas kernels, local(): pl.pallas_call(update_kernel, out_shape=jax.ShapeDtypeStruct((rows, cols)...  3.11 us

profile of v8, /device:TPU:20, one launch (start us, length us, event | category | flops | bytes accessed | tf_op | source)
XLA Modules:
  0.0 41.0 jit_solution(16518946244933188506)
XLA Ops:
  0.0 0.0 copy-start
  0.0 37.9 %panels.1 = (f32[640,256]{1,0:T(8,128)S(1)}, bf16[640,768]{1,0:T(8,128)(2,1)S(1)}, bf16[768,1280]{1,0:T(8,128)(2,1)S(1)}) custom-call(f32[640,1280]{1,0:T(8,128)} %a.3), custom_call_target="tpu_custom_call" | custom-call | tf_op jit(solution)/shard_map/panels/pallas_call | solution.py:448
  37.9 0.0 copy-done
  37.9 3.1 %update.1 = f32[640,1280]{1,0:T(8,128)} custom-call(f32[640,1280]{1,0:T(8,128)S(1)} %copy-done, f32[640,256]{1,0:T(8,128)S(1)} %get-tuple-element.8.panel, bf16[640,768]{1,0:T(8,128)(2,1)S(1)} %get-tuple-element.9.left, bf16[768,1280]{1,0:T(8,128)(2,1)S(1)} %get-tuple-element.10.right), custom_call_target="tpu_custom_call" | custom-call | tf_op jit(solution)/shard_map/update/pallas_call | solution.py:480
Async XLA Ops:
  0.0 37.9 %copy-start = (f32[640,1280]{1,0:T(8,128)S(1)}, f32[640,1280]{1,0:T(8,128)}, u32[]{:S(2)}) copy-start(f32[640,1280]{1,0:T(8,128)} %a.3) | copy-start | bytes 9830404

commit v9 on v8

--- a/solution.py
+++ b/solution.py
@@ -11,7 +11,7 @@
 NB = 128
 SUB = 8
 GROUP = 32
-CW = 128
+CW = 256
 TILE = 256
 MESH = pl.DeviceIdType.MESH
 f32 = jnp.float32
@@ -280,9 +280,6 @@
     def put(at, *step):
         places[min(int(at), 4 * half - 1)].append(functools.partial(*step))
 
-    put(0, direct_rest)
-    put(0, p_source, source & (c == 0), rest)
-    put(0, a_source)
     put(2, corner_rest)
     put(5, corner_pass)
     for t in range(nt):
@@ -293,9 +290,15 @@
             put(5 + 3 * t, p_pass, t, 0, 2)
     for t in range(na):
         for at in range(1, min(chips, 4)):
-            put(1.5 + 0.9 * t + 1.8 * (at - 1), a_pass, t, at)
-
-    opening()
+            put(2 + 1.8 * t + 2.6 * (at - 1), a_pass, t, at)
+
+    def begin():
+        opening()
+        direct_rest()
+        a_source()
+        p_source(source & (c == 0), rest)
+
+    begin()
 
     eye = jnp.where(
         lax.broadcasted_iota(jnp.int32, (NB, NB), 0) == lax.broadcasted_iota(jnp.int32, (NB, NB), 1),
@@ -403,7 +406,7 @@
         panel[:NB, NB:] = jnp.where(upper, aug[1, :, :NB], f32(0.0)).T
 
     ending.append(True)
-    opening()
+    begin()
     for steps in places:
         for step in steps:
             step()

time: 41.3 us -> 40 us (0.969)
  Pallas kernels: 41 us -> 39.5 us
    pallas_call x1, Pallas kernels: 37.9 us -> 36.4 us  [local(): pl.pallas_call(functools.partial(panels_kernel, nrow, ncol, rows, cols),...]
where the time goes in v9:
time: 40 us; the launch traced here: 39.5 us
  Pallas kernels  39.5 us (99%)
    pallas_call x1, Pallas kernels, local(): pl.pallas_call(functools.partial(panels_kernel, nrow, ncol, rows, cols),...  36.4 us
    pallas_call x1, Pallas kernels, local(): pl.pallas_call(update_kernel, out_shape=jax.ShapeDtypeStruct((rows, cols)...  3.1 us

profile of v9, /device:TPU:20, one launch (start us, length us, event | category | flops | bytes accessed | tf_op | source)
XLA Modules:
  0.0 39.5 jit_solution(14637210212008560596)
XLA Ops:
  0.0 0.0 copy-start
  0.0 36.4 %panels.1 = (f32[640,256]{1,0:T(8,128)S(1)}, bf16[640,768]{1,0:T(8,128)(2,1)S(1)}, bf16[768,1280]{1,0:T(8,128)(2,1)S(1)}) custom-call(f32[640,1280]{1,0:T(8,128)} %a.3), custom_call_target="tpu_custom_call" | custom-call | tf_op jit(solution)/shard_map/panels/pallas_call | solution.py:451
  36.4 0.0 copy-done
  36.4 3.1 %update.1 = f32[640,1280]{1,0:T(8,128)} custom-call(f32[640,1280]{1,0:T(8,128)S(1)} %copy-done, f32[640,256]{1,0:T(8,128)S(1)} %get-tuple-element.8.panel, bf16[640,768]{1,0:T(8,128)(2,1)S(1)} %get-tuple-element.9.left, bf16[768,1280]{1,0:T(8,128)(2,1)S(1)} %get-tuple-element.10.right), custom_call_target="tpu_custom_call" | custom-call | tf_op jit(solution)/shard_map/update/pallas_call | solution.py:483
Async XLA Ops:
  0.0 36.4 %copy-start = (f32[640,1280]{1,0:T(8,128)S(1)}, f32[640,1280]{1,0:T(8,128)}, u32[]{:S(2)}) copy-start(f32[640,1280]{1,0:T(8,128)} %a.3) | copy-start | bytes 9830404
